TPU v7x, 32 devices: a whole 2x2x4 slice. The times are simulated.
32 devices in a mesh: dp: 8 (over z, y), mp: 4 (over x, core).
Axes of the slice: x: 2, y: 2, z: 4, core: 2. Of those that a mesh axis runs over, the one named last changes fastest.
Arguments:
- inputs: bfloat16 [8192, 1024], P(('dp', 'mp')), may hold values from -6 to 6
- teacher: bfloat16 [8192, 1024], P(('dp', 'mp')), may hold values from -6 to 6
- segments: int32 [8, 1024], P('dp'), may hold values from 0 to 7, never falling along the last dimension, each value on 1 to 768 neighbouring positions
- valid_mask: int32 [8192], P(('dp', 'mp')), may hold values from 0 to 1, as said below
- qkv_copy: bfloat16 [1024, 3, 1024], P(None, None, 'mp'), may hold values from -0.1875 to 0.1875
- out_copy: bfloat16 [1024, 1024], P('mp'), may hold values from -0.5 to 0.5
- up_copy: bfloat16 [1024, 4096], P(None, 'mp'), may hold values from -0.1875 to 0.1875
- down_copy: bfloat16 [4096, 1024], P('mp'), may hold values from -0.09375 to 0.09375
- vector_copy: bfloat16 [12, 1024], replicated
- qkv_state: float32 [3, 1024, 3, 1024], P(None, 'dp', None, 'mp'), as said below
- out_state: float32 [3, 1024, 1024], P(None, 'mp', 'dp'), as said below
- up_state: float32 [3, 1024, 4096], P(None, 'dp', 'mp'), as said below
- down_state: float32 [3, 4096, 1024], P(None, 'mp', 'dp'), as said below
- vector_state: float32 [3, 12, 1024], replicated, as said below
Outputs:
- block_out: bfloat16 [8192, 1024], P(('dp', 'mp'))
- input_grad: float32 [8192, 1024], P(('dp', 'mp'))
- qkv_grad: float32 [1024, 3, 1024], P('dp', None, 'mp')
- out_grad: float32 [1024, 1024], P('mp', 'dp')
- up_grad: float32 [1024, 4096], P('dp', 'mp')
- down_grad: float32 [4096, 1024], P('mp', 'dp')
- vector_grad: float32 [12, 1024], replicated
- qkv_state_new: float32 [3, 1024, 3, 1024], P(None, 'dp', None, 'mp')
- out_state_new: float32 [3, 1024, 1024], P(None, 'mp', 'dp')
- up_state_new: float32 [3, 1024, 4096], P(None, 'dp', 'mp')
- down_state_new: float32 [3, 4096, 1024], P(None, 'mp', 'dp')
- vector_state_new: float32 [3, 12, 1024], replicated
- qkv_copy_new: bfloat16 [1024, 3, 1024], P(None, None, 'mp')
- out_copy_new: bfloat16 [1024, 1024], P('mp')
- up_copy_new: bfloat16 [1024, 4096], P(None, 'mp')
- down_copy_new: bfloat16 [4096, 1024], P('mp')
- vector_copy_new: bfloat16 [12, 1024], replicated
Inputs may be any that keep to these rules, and one draw needn't show every extreme that they name: `segments`: ids never fall along a sequence. `valid_mask`: the first token of every sequence is 1. `qkv_state`: row 2 is positive. `out_state`: row 2 is positive. `up_state`: row 2 is positive. `down_state`: row 2 is positive. `vector_state`: row 2 is positive.
All inputs are finite; a program needn't handle non-finite values.
Results may differ from a plain program's by a relative error of at most 0.007.
The roundings to bfloat16 on the way count: a program that leaves them out, or rounds other values in their place, can miss the bound.
Values may be sent and summed in bfloat16 or wider, within the bound.
A program may use at most 128 MiB of HBM per device.

v0:
```python
import math

import jax
import jax.numpy as jnp
from jax import lax
from jax.sharding import PartitionSpec as P

HEADS = 16
HD = 64
FF = 4096
LEN = 1024
BQ = 512


norm_eps = 1e-05
beta_one = 0.9
beta_two = 0.95
adam_eps = 1e-08
learn_rate = 0.001
decay_rate = 0.1
correction_one = 1.0 - (0.9**10) ** 10
correction_two = 1.0 - (0.95**10) ** 10
masked_value = -1e30


def gelu_tanh(operand):
    return (
        0.5
        * operand
        * (1.0 + jnp.tanh(0.7978845608 * (operand + 0.044715 * operand * operand * operand)))
    )


def norm_forward(operand, gain_row, shift_row):
    centred = operand - jnp.mean(operand, -1, keepdims=True)
    inverse = lax.rsqrt(jnp.mean(centred * centred, -1, keepdims=True) + norm_eps)
    normed = centred * inverse
    return (normed * gain_row + shift_row, normed, inverse)


def norm_backward(grad_out, normed, inverse, gain_row):
    scaled = grad_out * gain_row
    return inverse * (
        scaled
        - jnp.mean(scaled, -1, keepdims=True)
        - normed * jnp.mean(scaled * normed, -1, keepdims=True)
    )


def head_scores(block_query, key_heads, block_segments, segment_ids, first_row, slopes):
    score_scale = 1.0 / math.sqrt(HD)
    raw_scores = jnp.einsum(
        "qhd,khd->hqk", block_query, key_heads, preferred_element_type=jnp.float32
    )
    query_rows = first_row + jnp.arange(block_query.shape[0], dtype=jnp.int32)
    key_rows = jnp.arange(key_heads.shape[0], dtype=jnp.int32)
    distance = query_rows[:, None] - key_rows[None, :]
    allowed = (distance >= 0) & (block_segments[:, None] == segment_ids[None, :])
    scores = raw_scores * score_scale - slopes[:, None, None] * distance.astype(jnp.float32)[None]
    return jnp.where(allowed[None], scores, masked_value)


def block_layout(queries, segment_ids):
    block_count = LEN // BQ
    return (
        queries.reshape(block_count, BQ, queries.shape[1], queries.shape[2]),
        segment_ids.reshape(block_count, BQ),
        jnp.arange(block_count, dtype=jnp.int32) * BQ,
    )


def attend_sequence(queries, key_heads, value_heads, segment_ids, slopes):

    def one_block(block_item):
        block_query, block_segments, first_row = block_item
        scores = head_scores(block_query, key_heads, block_segments, segment_ids, first_row, slopes)
        row_top = jnp.max(scores, -1, keepdims=True)
        exponent = jnp.exp(scores - row_top)
        row_total = jnp.sum(exponent, -1, keepdims=True)
        low_probs = (exponent / row_total).astype(jnp.bfloat16)
        mixed_rows = jnp.einsum(
            "hqk,khd->qhd", low_probs, value_heads, preferred_element_type=jnp.float32
        )
        return (mixed_rows.astype(jnp.bfloat16), row_top, row_total)

    mixture, row_top, row_total = lax.map(one_block, block_layout(queries, segment_ids))
    return (mixture.reshape(queries.shape), row_top, row_total)


def attend_sequence_back(
    queries, key_heads, value_heads, segment_ids, grad_mixture, row_top, row_total, slopes
):
    score_scale = 1.0 / math.sqrt(HD)
    block_query_all, block_segment_all, first_rows = block_layout(queries, segment_ids)
    block_grad_all = grad_mixture.reshape(block_query_all.shape)

    def one_block(carried, block_item):
        grad_keys, grad_values = carried
        block_query, block_segments, first_row, block_grad, block_top, block_total = block_item
        scores = head_scores(block_query, key_heads, block_segments, segment_ids, first_row, slopes)
        probability = jnp.exp(scores - block_top) / block_total
        low_probs = probability.astype(jnp.bfloat16)
        grad_probs = jnp.einsum(
            "qhd,khd->hqk", block_grad, value_heads, preferred_element_type=jnp.float32
        )
        grad_values = grad_values + jnp.einsum(
            "hqk,qhd->khd", low_probs, block_grad, preferred_element_type=jnp.float32
        )
        inner_sum = jnp.sum(probability * grad_probs, -1, keepdims=True)
        grad_raw = (probability * (grad_probs - inner_sum) * score_scale).astype(jnp.bfloat16)
        grad_query = jnp.einsum(
            "hqk,khd->qhd", grad_raw, key_heads, preferred_element_type=jnp.float32
        ).astype(jnp.bfloat16)
        grad_keys = grad_keys + jnp.einsum(
            "hqk,qhd->khd", grad_raw, block_query, preferred_element_type=jnp.float32
        )
        return ((grad_keys, grad_values), grad_query)

    zero_keys = jnp.zeros(key_heads.shape, jnp.float32)
    block_items = (
        block_query_all,
        block_segment_all,
        first_rows,
        block_grad_all,
        row_top,
        row_total,
    )
    (grad_keys, grad_values), grad_queries = lax.scan(
        one_block, (zero_keys, zero_keys), block_items
    )
    return (
        grad_queries.reshape(queries.shape),
        grad_keys.astype(jnp.bfloat16),
        grad_values.astype(jnp.bfloat16),
    )


def split_heads(operand, sequences):
    return operand.reshape(sequences, LEN, operand.shape[1] // HD, HD)


def adam_update(gradient, stored, decay_factor, token_total):
    weight = stored[0]
    mean_grad = gradient / token_total
    moment_one = beta_one * stored[1] + (1.0 - beta_one) * mean_grad
    moment_two = beta_two * stored[2] + (1.0 - beta_two) * mean_grad * mean_grad
    update = (
        moment_one / correction_one / (jnp.sqrt(moment_two / correction_two) + adam_eps)
        + decay_factor * weight
    )
    weight = weight - learn_rate * update
    return (jnp.stack([weight, moment_one, moment_two]), weight.astype(jnp.bfloat16))


def shards(
    inputs,
    teacher,
    segments,
    valid_mask,
    qkv_copy,
    out_copy,
    up_copy,
    down_copy,
    vector_copy,
    qkv_state,
    out_state,
    up_state,
    down_state,
    vector_state,
):
    local_rows = inputs.shape[0]
    width = inputs.shape[1]
    sequences = segments.shape[0]
    all_rows = sequences * LEN
    model_index = lax.axis_index("mp")
    head_width = qkv_copy.shape[2]
    unit_width = up_copy.shape[1]
    local_heads = head_width // HD
    vectors = vector_copy.astype(jnp.float32)
    token_total = local_rows * lax.axis_size("dp") * lax.axis_size("mp")
    valid_float = valid_mask.astype(jnp.float32)
    token_count = lax.psum(jnp.sum(valid_float), ("dp", "mp"))
    loss_scale = token_total / token_count
    head_index = model_index * local_heads + jnp.arange(local_heads, dtype=jnp.int32)
    slopes = jnp.exp2(-8.0 * (head_index.astype(jnp.float32) + 1.0) / HEADS)
    query_bias = lax.dynamic_slice_in_dim(vectors[6], model_index * head_width, head_width)
    value_bias = lax.dynamic_slice_in_dim(vectors[7], model_index * head_width, head_width)
    unit_bias = lax.dynamic_slice_in_dim(
        vectors[8:].reshape(FF), model_index * unit_width, unit_width
    )
    source = inputs.astype(jnp.float32)
    norm_one, normed_one, inverse_one = norm_forward(source, vectors[0], vectors[1])
    first_rows = lax.all_gather(norm_one.astype(jnp.bfloat16), "mp", axis=0, tiled=True)
    projected = jnp.einsum("rd,dce->rce", first_rows, qkv_copy, preferred_element_type=jnp.float32)
    queries = (projected[:, 0] + query_bias).astype(jnp.bfloat16)
    key_heads = projected[:, 1].astype(jnp.bfloat16)
    value_heads = (projected[:, 2] + value_bias).astype(jnp.bfloat16)
    query_split = split_heads(queries, sequences)
    key_split = split_heads(key_heads, sequences)
    value_split = split_heads(value_heads, sequences)

    def attend_one(seq_item):
        return attend_sequence(seq_item[0], seq_item[1], seq_item[2], seq_item[3], slopes)

    mixture, row_top, row_total = lax.map(
        attend_one, (query_split, key_split, value_split, segments)
    )
    mixture = mixture.reshape(all_rows, head_width)
    attended = lax.psum_scatter(
        jnp.dot(mixture, out_copy, preferred_element_type=jnp.float32),
        "mp",
        scatter_dimension=0,
        tiled=True,
    )
    hidden = source + attended + vectors[2]
    norm_two, normed_two, inverse_two = norm_forward(hidden, vectors[3], vectors[4])
    second_rows = lax.all_gather(norm_two.astype(jnp.bfloat16), "mp", axis=0, tiled=True)
    up_value = jnp.dot(second_rows, up_copy, preferred_element_type=jnp.float32) + unit_bias
    activated, gelu_back = jax.vjp(gelu_tanh, up_value)
    activated_low = activated.astype(jnp.bfloat16)
    output = (
        hidden
        + lax.psum_scatter(
            jnp.dot(activated_low, down_copy, preferred_element_type=jnp.float32),
            "mp",
            scatter_dimension=0,
            tiled=True,
        )
        + vectors[5]
    )
    grad_output = valid_float[:, None] * (output - teacher.astype(jnp.float32)) * loss_scale
    grad_rows = lax.all_gather(grad_output.astype(jnp.bfloat16), "mp", axis=0, tiled=True)
    down_local = jnp.einsum(
        "rf,rd->fd", activated_low, grad_rows, preferred_element_type=jnp.float32
    )
    grad_act = jnp.einsum("rd,fd->rf", grad_rows, down_copy, preferred_element_type=jnp.float32)
    grad_up = gelu_back(grad_act)[0].astype(jnp.bfloat16)
    up_local = jnp.einsum("rd,rf->df", second_rows, grad_up, preferred_element_type=jnp.float32)
    unit_bias_grad = jnp.sum(grad_up.astype(jnp.float32), 0)
    grad_second = lax.psum_scatter(
        jnp.einsum("rf,df->rd", grad_up, up_copy, preferred_element_type=jnp.float32),
        "mp",
        scatter_dimension=0,
        tiled=True,
    )
    grad_hidden = grad_output + norm_backward(grad_second, normed_two, inverse_two, vectors[3])
    hidden_rows = lax.all_gather(grad_hidden.astype(jnp.bfloat16), "mp", axis=0, tiled=True)
    out_local = jnp.einsum("rf,rd->fd", mixture, hidden_rows, preferred_element_type=jnp.float32)
    grad_mixture = jnp.einsum(
        "rd,fd->rf", hidden_rows, out_copy, preferred_element_type=jnp.float32
    ).astype(jnp.bfloat16)

    def attend_back(seq_item):
        return attend_sequence_back(
            seq_item[0],
            seq_item[1],
            seq_item[2],
            seq_item[3],
            seq_item[4],
            seq_item[5],
            seq_item[6],
            slopes,
        )

    grad_queries, grad_keys, grad_values = lax.map(
        attend_back,
        (
            query_split,
            key_split,
            value_split,
            segments,
            split_heads(grad_mixture, sequences),
            row_top,
            row_total,
        ),
    )
    stacked = jnp.stack(
        [
            grad_queries.reshape(all_rows, head_width),
            grad_keys.reshape(all_rows, head_width),
            grad_values.reshape(all_rows, head_width),
        ],
        1,
    )
    qkv_local = jnp.einsum("rd,rce->dce", first_rows, stacked, preferred_element_type=jnp.float32)
    query_bias_grad = jnp.sum(stacked[:, 0].astype(jnp.float32), 0)
    value_bias_grad = jnp.sum(stacked[:, 2].astype(jnp.float32), 0)
    grad_first = lax.psum_scatter(
        jnp.einsum("rce,dce->rd", stacked, qkv_copy, preferred_element_type=jnp.float32),
        "mp",
        scatter_dimension=0,
        tiled=True,
    )
    input_grad = grad_hidden + norm_backward(grad_first, normed_one, inverse_one, vectors[0])
    placed_query = lax.dynamic_update_slice_in_dim(
        jnp.zeros((width,), jnp.float32), query_bias_grad, model_index * head_width, 0
    )
    placed_value = lax.dynamic_update_slice_in_dim(
        jnp.zeros((width,), jnp.float32), value_bias_grad, model_index * head_width, 0
    )
    placed_units = lax.dynamic_update_slice_in_dim(
        jnp.zeros((FF,), jnp.float32), unit_bias_grad, model_index * unit_width, 0
    ).reshape(FF // width, width)
    norm_terms = jnp.stack(
        [
            jnp.sum(grad_first * normed_one, 0),
            jnp.sum(grad_first, 0),
            jnp.sum(grad_hidden, 0),
            jnp.sum(grad_second * normed_two, 0),
            jnp.sum(grad_second, 0),
            jnp.sum(grad_output, 0),
            placed_query,
            placed_value,
        ]
    )
    vector_grad = lax.psum(jnp.concatenate([norm_terms, placed_units], 0), ("dp", "mp"))
    qkv_grad, out_grad, up_grad, down_grad = (
        lax.psum_scatter(qkv_local, "dp", scatter_dimension=0, tiled=True),
        lax.psum_scatter(out_local, "dp", scatter_dimension=1, tiled=True),
        lax.psum_scatter(up_local, "dp", scatter_dimension=0, tiled=True),
        lax.psum_scatter(down_local, "dp", scatter_dimension=1, tiled=True),
    )
    qkv_new, qkv_low = adam_update(qkv_grad, qkv_state, decay_rate, token_total)
    out_new, out_low = adam_update(out_grad, out_state, decay_rate, token_total)
    up_new, up_low = adam_update(up_grad, up_state, decay_rate, token_total)
    down_new, down_low = adam_update(down_grad, down_state, decay_rate, token_total)
    vector_new, vector_low = adam_update(vector_grad, vector_state, 0.0, token_total)
    qkv_full, out_full, up_full, down_full = (
        lax.all_gather(qkv_low, "dp", axis=0, tiled=True),
        lax.all_gather(out_low, "dp", axis=1, tiled=True),
        lax.all_gather(up_low, "dp", axis=0, tiled=True),
        lax.all_gather(down_low, "dp", axis=1, tiled=True),
    )
    return (
        output.astype(jnp.bfloat16),
        input_grad,
        qkv_grad,
        out_grad,
        up_grad,
        down_grad,
        vector_grad,
        qkv_new,
        out_new,
        up_new,
        down_new,
        vector_new,
        qkv_full,
        out_full,
        up_full,
        down_full,
        vector_low,
    )


def solution(mesh):
    in_specs = (
        P(("dp", "mp"), None),
        P(("dp", "mp"), None),
        P("dp", None),
        P(("dp", "mp")),
        P(None, None, "mp"),
        P("mp", None),
        P(None, "mp"),
        P("mp", None),
        P(),
        P(None, "dp", None, "mp"),
        P(None, "mp", "dp"),
        P(None, "dp", "mp"),
        P(None, "mp", "dp"),
        P(),
    )
    out_specs = (
        P(("dp", "mp"), None),
        P(("dp", "mp"), None),
        P("dp", None, "mp"),
        P("mp", "dp"),
        P("dp", "mp"),
        P("mp", "dp"),
        P(),
        P(None, "dp", None, "mp"),
        P(None, "mp", "dp"),
        P(None, "dp", "mp"),
        P(None, "mp", "dp"),
        P(),
        P(None, None, "mp"),
        P("mp", None),
        P(None, "mp"),
        P("mp", None),
        P(),
    )
    return jax.shard_map(shards, mesh=mesh, in_specs=in_specs, out_specs=out_specs, check_vma=False)
```

profile of v0, /device:TPU:0, one launch (start us, length us, event | category | flops | bytes accessed | tf_op | source)
XLA Modules:
  0.0 865.0 jit_solution(4086745193280031015)
XLA Ops:
  15.9 23.3 %all-gather.8.cloned.1.call-done = bf16[1024,1024]{1,0:T(8,128)(2,1)} async-done(((bf16[256,1024]{1,0:T(8,128)(2,1)}), bf16[1024,1024]{1,0:T(8,128)(2,1)}) %all-gather.8.cloned.1.call-update) | async-done | bytes 2097168 | tf_op jit(solution)/shard_map/all_gather | solution.py:193
  39.1 3.9 fusion.80
  50.6 25.0 %while.52 = (s32[]{:T(128)}, bf16[2,512,4,64]{1,3,2,0:T(8,128)(2,1)S(1)}, f32[2,4,512,1]{2,1,3,0:T(4,128)S(1)}, f32[2,4,512,1]{2,1,3,0:T(4,128)S(1)}, s32[2]{0:T...) while((s32[]{:T(128)}, ...), condition=%wide.region_5.6_spmd.clone, body=%wide.region_2.5_spmd.clone.sunk | while | flops 577892864 | bytes 37315280 | solution.py:86
  52.8 3.9 fusion.190
  56.7 3.0 fusion.191
  59.7 3.4 fusion.192
  65.3 3.9 fusion.190
  69.2 3.0 fusion.191
  72.2 3.4 fusion.192
  77.0 3.7 fusion.135
  80.8 44.6 %reduce-scatter.9.cloned.1.call-done = f32[256,1024]{1,0:T(8,128)} async-done(((f32[1024,1024]{1,0:T(8,128)}), f32[256,1024]{1,0:T(8,128)}) %reduce-scatter.9.cloned.1.call-update) | async-done | bytes 1048592 | tf_op jit(solution)/shard_map/reduce_scatter | solution.py:209
  128.4 11.2 %reduce-scatter.11.cloned.1.call-start = ((), (), s32[]{:S(2)}) async-start(), calls=%async_computation.11 | async-start | bytes 5242880 | tf_op jit(solution)/shard_map/reduce_scatter | solution.py:223
  139.7 11.4 %all-gather.10.cloned.1.call-done = bf16[1024,1024]{1,0:T(8,128)(2,1)} async-done(((bf16[256,1024]{1,0:T(8,128)(2,1)}), bf16[1024,1024]{1,0:T(8,128)(2,1)}) %all-gather.10.cloned.1.call-update) | async-done | bytes 2097168 | tf_op jit(solution)/shard_map/all_gather | solution.py:217
  151.1 4.5 fusion.136
  157.6 4.7 fusion.122
  163.6 39.8 %psum.14 = f32[]{:T(128)} all-reduce(f32[]{:T(128)} %convert_reduce_fusion.4), channel_id=1, replica_groups=mesh['dp'=8,'mp'=4] {'dp','mp'}, use_global_device_ids=true, to_apply=%region_11.12 | all-reduce | flops 1 | bytes 8 | tf_op jit(solution)/shard_map/psum | solution.py:182
  204.1 3.6 reduce-scatter.11.cloned.1.call-done
  207.7 3.0 fusion.129
  212.7 22.7 %all-gather.12.cloned.1.call-done = bf16[1024,1024]{1,0:T(8,128)(2,1)} async-done(((bf16[256,1024]{1,0:T(8,128)(2,1)}), bf16[1024,1024]{1,0:T(8,128)(2,1)}) %all-gather.12.cloned.1.call-update) | async-done | bytes 2097168 | tf_op jit(solution)/shard_map/all_gather | solution.py:232
  235.4 8.7 %convert_reduce_fusion = (f32[1024]{0:T(1024)}, bf16[1024,1024]{1,0:T(8,128)(2,1)S(1)}) fusion(f32[1024,1024]{1,0:T(8,128)} %copy-done.34, f32[1024]{0:T(1024)S(1)} %dynamic_slice.67, bf16[1024,1024]{1,0:T(8,128)(2,1)} %all-gather.12.cloned.1.call-done, bf16[1024,1024]{1,0:T(8,128)(2,1)S(1)} %copy-done), kind=kOutput, calls=%fused_computation.78 | convolution fusion | flops 2175794176 | bytes 10493952 | tf_op jit(solution)/shard_map/rd,fd->rf/dot_general | solution.py:236
  245.4 4.3 fusion.137
  249.8 44.6 %reduce-scatter.13.cloned.1.call-done = f32[256,1024]{1,0:T(8,128)} async-done(((f32[1024,1024]{1,0:T(8,128)}), f32[256,1024]{1,0:T(8,128)}) %reduce-scatter.13.cloned.1.call-update) | async-done | bytes 1048592 | tf_op jit(solution)/shard_map/reduce_scatter | solution.py:240
  299.9 7.9 fusion.121
  307.9 6.6 fusion.139
  314.9 7.7 all-gather.14.cloned.1.call-done
  322.6 3.1 convolution_convert_fusion
  328.5 82.2 %while.53 = (s32[]{:T(128)}, f32[1024,4,64]{0,2,1:T(8,128)}, f32[1024,4,64]{0,2,1:T(8,128)S(1)}, bf16[2,512,4,64]{1,3,2,0:T(8,128)(2,1)S(1)}, bf16[2,512,4,64]{1...) while((s32[]{:T(128)}, f32[1024,4,64]{0,2,1:T(8,128)}, ...), condition=%wide.region_17.18_spmd.clone, body=%wide.region_15.17_spmd.clone.sunk | while | flops 1382160896 | bytes 140312896 | solution.py:128
  330.7 4.4 exponential_divide_fusion.2
  338.3 4.5 fusion.205
  342.8 13.1 %fusion.208 = bf16[2,512,4,64]{1,3,2,0:T(8,128)(2,1)S(1)} fusion(bf16[2,512,4,64]{1,3,2,0:T(8,128)(2,1)S(1)} %get-tuple-element.646, s32[]{:T(128)S(6)} %copy.82, bf16[1024,4,64]{0,2,1:T(8,128)(2,1)S(1)} %copy-done.16, f32[4,512,1024]{2,1,0:T(8,128)} %copy-done.2, f32[4,512,1024]{2,1,0:T(8,128)} %fusion.205), kind=kOutput, calls=%fused_computation.45.clone.1 | convolution fusion | flops 279055360 | bytes 34340868 | tf_op jit(solution)/shard_map/while/body/eval_jaxpr/while/body/eval_jaxpr/hqk,khd->qhd/dot_general | solution.py:111
  355.9 13.8 %fusion.206 = f32[1024,4,64]{0,2,1:T(8,128)} fusion(f32[4,512,1024]{2,1,0:T(8,128)} %copy-done.2, f32[4,512,1024]{2,1,0:T(8,128)} %fusion.205, f32[1024,4,64]{0,2,1:T(8,128)} %get-tuple-element.644, pred[]{:T(512)S(6)} %compare.3, bf16[2,512,4,64]{1,3,2,0:T(8,128)(2,1)} %get-tuple-element.663, s32[]{:T(128)S(6)} %copy.82), kind=kOutput, calls=%fused_computation.42.clone.1 | convolution fusion | flops 279448576 | bytes 35913732 | tf_op jit(solution)/shard_map/while/body/eval_jaxpr/while/body/eval_jaxpr/hqk,qhd->khd/dot_general | solution.py:114
  371.9 4.4 exponential_divide_fusion.2
  379.6 4.5 fusion.205
  384.1 12.7 %fusion.208 = bf16[2,512,4,64]{1,3,2,0:T(8,128)(2,1)S(1)} fusion(bf16[2,512,4,64]{1,3,2,0:T(8,128)(2,1)S(1)} %get-tuple-element.646, s32[]{:T(128)S(6)} %copy.82, bf16[1024,4,64]{0,2,1:T(8,128)(2,1)S(1)} %copy-done.16, f32[4,512,1024]{2,1,0:T(8,128)} %copy-done.2, f32[4,512,1024]{2,1,0:T(8,128)} %fusion.205), kind=kOutput, calls=%fused_computation.45.clone.1 | convolution fusion | flops 279055360 | bytes 34340868 | tf_op jit(solution)/shard_map/while/body/eval_jaxpr/while/body/eval_jaxpr/hqk,khd->qhd/dot_general | solution.py:111
  396.8 13.9 %fusion.206 = f32[1024,4,64]{0,2,1:T(8,128)} fusion(f32[4,512,1024]{2,1,0:T(8,128)} %copy-done.2, f32[4,512,1024]{2,1,0:T(8,128)} %fusion.205, f32[1024,4,64]{0,2,1:T(8,128)} %get-tuple-element.644, pred[]{:T(512)S(6)} %compare.3, bf16[2,512,4,64]{1,3,2,0:T(8,128)(2,1)} %get-tuple-element.663, s32[]{:T(128)S(6)} %copy.82), kind=kOutput, calls=%fused_computation.42.clone.1 | convolution fusion | flops 279448576 | bytes 35913732 | tf_op jit(solution)/shard_map/while/body/eval_jaxpr/while/body/eval_jaxpr/hqk,qhd->khd/dot_general | solution.py:114
  415.6 5.4 fusion.78
  423.9 83.9 %reduce-scatter.21.cloned.1.call-done = f32[128,1024]{1,0:T(8,128)} async-done(((f32[1024,1024]{1,0:T(8,128)}), f32[128,1024]{1,0:T(8,128)}) %reduce-scatter.21.cloned.1.call-update) | async-done | bytes 524304 | tf_op jit(solution)/shard_map/reduce_scatter | solution.py:320
  507.8 2.9 fusion.125
  510.8 3.3 fusion.138
  514.2 5.6 convolution_bitcast_fusion
  519.9 67.3 %reduce-scatter.17.cloned.1.call-done = f32[128,3,256]{2,0,1:T(8,128)} async-done(((f32[1024,3,256]{2,0,1:T(8,128)}), f32[128,3,256]{2,0,1:T(8,128)}) %reduce-scatter.17.cloned.1.call-update) | async-done | bytes 393232 | tf_op jit(solution)/shard_map/reduce_scatter | solution.py:318
  596.9 42.8 %all-gather.20.cloned.1.call-done = bf16[1024,1024]{1,0:T(8,128)(2,1)} async-done(((bf16[1024,128]{1,0:T(8,128)(2,1)}), bf16[1024,1024]{1,0:T(8,128)(2,1)}) %all-gather.20.cloned.1.call-update) | async-done | bytes 2097168 | tf_op jit(solution)/shard_map/all_gather | solution.py:332
  639.7 50.3 %all-gather.18.cloned.1.call-done = bf16[1024,1024]{1,0:T(8,128)(2,1)} async-done(((bf16[128,1024]{1,0:T(8,128)(2,1)}), bf16[1024,1024]{1,0:T(8,128)(2,1)}) %all-gather.18.cloned.1.call-update) | async-done | bytes 2097168 | tf_op jit(solution)/shard_map/all_gather | solution.py:331
  690.0 66.7 %reduce-scatter.19.cloned.1.call-done = f32[256,128]{1,0:T(8,128)} async-done(((f32[256,1024]{1,0:T(8,128)}), f32[256,128]{1,0:T(8,128)}) %reduce-scatter.19.cloned.1.call-update) | async-done | bytes 131088 | tf_op jit(solution)/shard_map/reduce_scatter | solution.py:319
  757.9 27.1 %all_gather.29 = bf16[256,1024]{1,0:T(8,128)(2,1)S(1)} all-gather(bf16[256,128]{1,0:T(8,128)(2,1)S(1)} %get-tuple-element.384), channel_id=1, replica_groups=mesh['dp'=8,'mp'=4] {'dp'}, dimensions={1}, use_global_device_ids=true | all-gather | bytes 589824 | tf_op jit(solution)/shard_map/all_gather | solution.py:330
  787.9 14.7 %reduce-scatter.15.cloned.1.call-done = f32[256,1024]{1,0:T(8,128)} async-done(((f32[1024,1024]{1,0:T(8,128)}), f32[256,1024]{1,0:T(8,128)}) %reduce-scatter.15.cloned.1.call-update) | async-done | bytes 1048592 | tf_op jit(solution)/shard_map/reduce_scatter | solution.py:288
  805.9 40.4 %psum.15 = f32[12,1024]{1,0:T(8,128)S(1)} all-reduce(f32[12,1024]{1,0:T(8,128)S(1)} %concatenate.3), channel_id=1, replica_groups=mesh['dp'=8,'mp'=4] {'dp','mp'}, use_global_device_ids=true, to_apply=%region_34.35 | all-reduce | flops 12288 | bytes 98304 | tf_op jit(solution)/shard_map/psum | solution.py:316
  853.8 3.1 copy.99
  (215 shorter events, 84.5 us)
Async XLA Ops:
  7.2 150.4 %copy-start = (bf16[1024,1024]{1,0:T(8,128)(2,1)S(1)}, bf16[1024,1024]{1,0:T(8,128)(2,1)}, u32[]{:S(2)}) copy-start(bf16[1024,1024]{1,0:T(8,128)(2,1)} %param.25) | copy-start | bytes 6291460
  7.2 31.9 %all-gather.8.cloned.1.call-start = ((), (), s32[]{:S(2)}) async-start(), calls=%async_computation.8 | async-start | bytes 2621440 | tf_op jit(solution)/shard_map/all_gather | solution.py:193
  8.6 2.4 copy-start.24
  9.9 33.1 %copy-start.30 = (f32[256]{0:T(256)}, f32[256]{0:T(256)S(1)}, u32[]{:S(2)}) copy-start(f32[256]{0:T(256)S(1)} %add_rsqrt_fusion.1) | copy-start | bytes 3076
  13.7 111.7 %reduce-scatter.9.cloned.1.call-start = ((), (), s32[]{:S(2)}) async-start(), calls=%async_computation.9 | async-start | bytes 5242880 | tf_op jit(solution)/shard_map/reduce_scatter | solution.py:209
  43.9 6.7 copy-start.18
  75.6 5.1 copy-start.3
  80.7 58.8 %copy-start.21 = (bf16[12,1024]{1,0:T(8,128)(2,1)S(1)}, bf16[12,1024]{1,0:T(8,128)(2,1)}, u32[]{:S(2)}) copy-start(bf16[12,1024]{1,0:T(8,128)(2,1)} %param.26) | copy-start | bytes 73732
  80.8 70.3 %all-gather.10.cloned.1.call-start = ((), (), s32[]{:S(2)}) async-start(), calls=%async_computation.10 | async-start | bytes 2621440 | tf_op jit(solution)/shard_map/all_gather | solution.py:217
  128.4 79.3 %reduce-scatter.11.cloned.1.call-start = ((), (), s32[]{:S(2)}) async-start(), calls=%async_computation.11 | async-start | bytes 5242880 | tf_op jit(solution)/shard_map/reduce_scatter | solution.py:223
  155.7 1.9 copy-start.34
  162.4 73.0 %all-gather.12.cloned.1.call-start = ((), (), s32[]{:S(2)}) async-start(), calls=%async_computation.12 | async-start | bytes 2621440 | tf_op jit(solution)/shard_map/all_gather | solution.py:232
  212.6 81.8 %reduce-scatter.13.cloned.1.call-start = ((), (), s32[]{:S(2)}) async-start(), calls=%async_computation.13 | async-start | bytes 5242880 | tf_op jit(solution)/shard_map/reduce_scatter | solution.py:240
  235.4 10.0 %copy-start.33 = (bf16[1024,1024]{1,0:T(8,128)(2,1)S(1)}, bf16[1024,1024]{1,0:T(8,128)(2,1)}, u32[]{:S(2)}) copy-start(bf16[1024,1024]{1,0:T(8,128)(2,1)} %param.24) | copy-start | bytes 6291460
  249.7 47.0 %copy-start.9 = (f32[256,1024]{1,0:T(8,128)S(1)}, f32[256,1024]{1,0:T(8,128)}, u32[]{:S(2)}) copy-start(f32[256,1024]{1,0:T(8,128)} %copy-done.8) | copy-start | bytes 3145732
  249.7 72.9 %all-gather.14.cloned.1.call-start = ((), (), s32[]{:S(2)}) async-start(), calls=%async_computation.14 | async-start | bytes 2621440 | tf_op jit(solution)/shard_map/all_gather | solution.py:247
  298.9 8.9 %copy-start.6 = (f32[256,1024]{1,0:T(8,128)}, f32[256,1024]{1,0:T(8,128)S(1)}, u32[]{:S(2)}) copy-start(f32[256,1024]{1,0:T(8,128)S(1)} %get-tuple-element.395) | copy-start | bytes 3145732
  299.9 121.2 %reduce-scatter.23.cloned.1.call-start = ((), (), s32[]{:S(2)}) async-start(), calls=%async_computation.19 | async-start | bytes 4718592 | tf_op jit(solution)/shard_map/reduce_scatter | solution.py:321
  307.8 200.0 %reduce-scatter.21.cloned.1.call-start = ((), (), s32[]{:S(2)}) async-start(), calls=%async_computation.18 | async-start | bytes 4718592 | tf_op jit(solution)/shard_map/reduce_scatter | solution.py:320
  314.5 8.2 copy-start.14
  314.5 14.0 %copy-start.4 = (bf16[1024,4,64]{0,2,1:T(8,128)(2,1)S(1)}, bf16[1024,4,64]{0,2,1:T(8,128)(2,1)}, u32[]{:S(2)}) copy-start(bf16[1024,4,64]{0,2,1:T(8,128)(2,1)} %copy-done.3) | copy-start | bytes 1572868
  314.5 272.7 %reduce-scatter.17.cloned.1.call-start = ((), (), s32[]{:S(2)}) async-start(), calls=%async_computation.16 | async-start | bytes 3538944 | tf_op jit(solution)/shard_map/reduce_scatter | solution.py:318
  335.1 3.2 copy-start.2
  338.3 4.5 copy-start.16
  376.3 3.2 copy-start.2
  379.6 4.5 copy-start.16
  414.6 6.4 copy-start.15
  415.6 5.4 copy-start.17
  421.0 89.8 %copy-start.11 = (bf16[32,8,2,512]{3,1,2,0:T(8,128)(2,1)S(1)}, bf16[32,8,2,512]{3,1,2,0:T(8,128)(2,1)}, u32[]{:S(2)}) copy-start(bf16[32,8,2,512]{3,1,2,0:T(8,128)(2,1)} %copy-done.10) | copy-start | bytes 1572868
  421.0 218.7 %all-gather.20.cloned.1.call-start = ((), (), s32[]{:S(2)}) async-start(), calls=%async_computation.22 | async-start | bytes 2359296 | tf_op jit(solution)/shard_map/all_gather | solution.py:332
  423.8 266.1 %all-gather.18.cloned.1.call-start = ((), (), s32[]{:S(2)}) async-start(), calls=%async_computation.21 | async-start | bytes 2359296 | tf_op jit(solution)/shard_map/all_gather | solution.py:331
  510.8 245.9 %reduce-scatter.19.cloned.1.call-start = ((), (), s32[]{:S(2)}) async-start(), calls=%async_computation.17 | async-start | bytes 1179648 | tf_op jit(solution)/shard_map/reduce_scatter | solution.py:319
  514.1 288.5 %reduce-scatter.15.cloned.1.call-start = ((), (), s32[]{:S(2)}) async-start(), calls=%async_computation.15 | async-start | bytes 5242880 | tf_op jit(solution)/shard_map/reduce_scatter | solution.py:288
  519.8 69.9 %copy-start.31 = (f32[1024]{0:T(1024)S(1)}, f32[1024]{0:T(1024)}, u32[]{:S(2)}) copy-start(f32[1024]{0:T(1024)} %get-tuple-element.388) | copy-start | bytes 12292
  519.8 330.4 %all-gather.16.cloned.1.call-start = ((), (), s32[]{:S(2)}) async-start(), calls=%async_computation.20 | async-start | bytes 1769472 | tf_op jit(solution)/shard_map/all_gather | solution.py:329
  591.9 193.9 %copy-start.13 = (f32[1,128,3,256]{3,1,2,0:T(8,128)S(1)}, f32[1,128,3,256]{3,1,2,0:T(8,128)}, u32[]{:S(2)}) copy-start(f32[1,128,3,256]{3,1,2,0:T(8,128)} %get-tuple-element.411) | copy-start | bytes 1179652
  591.9 210.7 %copy-start.5 = (bf16[256,1024]{1,0:T(8,128)(2,1)S(1)}, bf16[256,1024]{1,0:T(8,128)(2,1)}, u32[]{:S(2)}) copy-start(bf16[256,1024]{1,0:T(8,128)(2,1)} %param.18) | copy-start | bytes 1572868
  591.9 210.7 %copy-start.23 = (f32[1,1024]{1,0:T(1,128)S(1)}, f32[1,1024]{1,0:T(1,128)}, u32[]{:S(2)}) copy-start(f32[1,1024]{1,0:T(1,128)} %copy-done.22) | copy-start | bytes 12292
  591.9 210.7 %copy-start.25 = (f32[256]{0:T(256)S(1)}, f32[256]{0:T(256)}, u32[]{:S(2)}) copy-start(f32[256]{0:T(256)} %copy-done.24) | copy-start | bytes 3076
  594.5 209.9 %copy-start.26 = (f32[1024]{0:T(1024)S(1)}, f32[1024]{0:T(1024)}, u32[]{:S(2)}) copy-start(f32[1024]{0:T(1024)} %get-tuple-element.392) | copy-start | bytes 12292
  594.5 209.9 %copy-start.27 = (f32[1024]{0:T(1024)S(1)}, f32[1024]{0:T(1024)}, u32[]{:S(2)}) copy-start(f32[1024]{0:T(1024)} %get-tuple-element.320) | copy-start | bytes 12292
  594.5 251.8 %copy-start.20 = (f32[3,12,1024]{2,1,0:T(8,128)S(1)}, f32[3,12,1024]{2,1,0:T(8,128)}, u32[]{:S(2)}) copy-start(f32[3,12,1024]{2,1,0:T(8,128)} %param.31) | copy-start | bytes 442372
  594.5 253.2 %copy-start.7 = (f32[256,1024]{1,0:T(8,128)S(1)}, f32[256,1024]{1,0:T(8,128)}, u32[]{:S(2)}) copy-start(f32[256,1024]{1,0:T(8,128)} %copy-done.6) | copy-start | bytes 3145732
  596.9 93.1 %copy-start.28 = (f32[1,1024]{1,0:T(1,128)}, f32[1,1024]{1,0:T(1,128)S(1)}, u32[]{:S(2)}) copy-start(f32[1,1024]{1,0:T(1,128)S(1)} %constant_dynamic-update-slice_fusion) | copy-start | bytes 12292
  785.0 19.4 %copy-start.29 = (f32[1,1024]{1,0:T(1,128)S(1)}, f32[1,1024]{1,0:T(1,128)}, u32[]{:S(2)}) copy-start(f32[1,1024]{1,0:T(1,128)} %copy-done.28) | copy-start | bytes 12292
  846.3 7.6 copy-start.19
  850.2 6.7 copy-start.12
  853.0 5.2 copy-start.1
  (5 other events, 4.4 us)
Sparse Core Ops, SparseCore 0:
  13.8 25.2 all-gather.7
  80.9 44.4 reduce-scatter.8
  128.5 22.5 all-gather.9
  162.5 45.1 reduce-scatter.10
  212.7 22.5 all-gather.11
  249.9 44.4 reduce-scatter.12
  300.0 22.5 all-gather.13
  327.3 88.4 reduce-scatter.22
  420.0 87.7 reduce-scatter.20
  512.3 74.8 reduce-scatter.16
  589.4 50.2 all-gather.19
  642.4 47.4 all-gather.17
  694.3 62.3 reduce-scatter.18
  759.1 43.4 reduce-scatter.14
  805.4 44.6 all-gather.15
where the time goes:
time: 874 us; the launch traced here: 865 us
  waiting for transfers between devices  484 us (55%)
  matrix products  150 us (17%)
  blocking collectives  107 us (12%)
  other arithmetic  58.6 us (7%)
  local copies, waits for them, and re-layouts  37.6 us (4%)
  between operations  15.3 us (2%)
  starting transfers between devices  12.2 us (1%)
    reduce_scatter x1, waiting for transfers between devices, shards(): lax.psum_scatter(up_local, 'dp', scatter_dimension=0, tiled=True)  83.9 us
    reduce_scatter x1, waiting for transfers between devices, shards(): lax.psum_scatter(qkv_local, 'dp', scatter_dimension=0, tiled=True)  67.3 us
    reduce_scatter x1, waiting for transfers between devices, shards(): lax.psum_scatter(out_local, 'dp', scatter_dimension=1, tiled=True)  66.7 us
    all_gather x1, waiting for transfers between devices, shards(): lax.all_gather(up_low, 'dp', axis=0, tiled=True)  50.3 us
    reduce_scatter x1, waiting for transfers between devices, shards(): lax.psum_scatter(jnp.einsum('rf,df->rd', grad_up, up_copy, preferred_elem...  44.6 us
    reduce_scatter x1, waiting for transfers between devices, shards(): lax.psum_scatter(jnp.dot(mixture, out_copy, preferred_element_type=jnp.fl...  44.6 us
    all_gather x1, waiting for transfers between devices, shards(): lax.all_gather(down_low, 'dp', axis=1, tiled=True)  42.8 us
    psum x1, blocking collectives, shards(): lax.psum(jnp.concatenate([norm_terms, placed_units], 0), ('dp', 'mp'))  40.4 us
  transfers between devices with their start and end apart: 15, of which 13 were waited for; matrix products, arithmetic and copies ran while one was open for 17% of the time, Pallas kernels for 0%

commit v1 on v0

v1 whole, which is shorter than its diff:
```python
import functools
import math

import jax
import jax.numpy as jnp
from jax import lax
from jax.experimental import pallas as pl
from jax.experimental.pallas import tpu as pltpu
from jax.sharding import PartitionSpec as P

HEADS = 16
HD = 64

norm_eps = 1e-05
beta_one = 0.9
beta_two = 0.95
adam_eps = 1e-08
learn_rate = 0.001
decay_rate = 0.1
correction_one = 1.0 - (0.9**10) ** 10
correction_two = 1.0 - (0.95**10) ** 10
log2_e = 1.4426950408889634

CHUNKS = 2
BQ = 256
TILE = 256
MESH = pl.DeviceIdType.MESH
F32 = jnp.float32
BF16 = jnp.bfloat16
NN = ((1,), (0,))
NT = ((1,), (1,))
TN = ((0,), (0,))


def mm(a, b, dims):
    return lax.dot_general(a, b, (dims, ((), ())), preferred_element_type=F32)


def gelu_both(v):
    c = 0.7978845608
    v2 = v * v
    th = jnp.tanh(c * (v + 0.044715 * v2 * v))
    half = 0.5 * (1.0 + th)
    back = half + 0.5 * v * (1.0 - th * th) * (c * (1.0 + 3.0 * 0.044715 * v2))
    return v * half, back


def norm_rows(v):
    centred = v - jnp.mean(v, -1, keepdims=True)
    inverse = lax.rsqrt(jnp.mean(centred * centred, -1, keepdims=True) + norm_eps)
    return centred * inverse, inverse


def norm_backward(grad_out, normed, inverse, gain_row):
    scaled = grad_out * gain_row
    return inverse * (
        scaled
        - jnp.mean(scaled, -1, keepdims=True)
        - normed * jnp.mean(scaled * normed, -1, keepdims=True)
    )


def block_kernel(
    sizes,
    x_ref, t_ref, segr_ref, segc_ref, valid_ref, vec_ref,
    wqkv_hbm, wout_hbm, wup_hbm, wdown_hbm,
    bo_ref, ig_ref, vg_ref, dqkv_hbm, dout_hbm, dup_hbm, ddown_hbm,
    wqkv, wout, wup, wdown, w_sem,
    g1, g2, g3, g4, qkv, qT, kT, vT, mixT, mix, lse, dist,
    hidden, n1, n2, inv1, inv2, go, act, gelub, gup,
    gm, gmT, gk, gv, gqT, st,
    tmp, keep, rs_cs, rs_cr, rs_xs, rs_xr,
    cnt, cnt_r, stage, stage_sem,
    ag_ss, ag_rs, rs_ss, rs_rs, cnt_ss, cnt_rs,
):
    dp_size, mp_size = sizes
    dp = lax.axis_index("dp")
    m = lax.axis_index("mp")
    core = lax.rem(m, 2)
    chip = m // 2
    mc = m + 1 - 2 * core
    mx = lax.rem(m + 2, 4)
    md = mc + mx - m
    C = CHUNKS
    R, D = x_ref.shape
    rc = R // C
    T = mp_size * R
    HW = wout.shape[0]
    FU = wup.shape[1]

    bits = []
    for b in range(mp_size.bit_length() - 1):
        bits.append(("mp", b))
    for b in range(dp_size.bit_length() - 1):
        bits.append(("dp", b))

    def flip(v, b):
        w = 1 << b
        return v + w - 2 * w * lax.rem(v // w, 2)

    def bit_partner(item):
        axis, b = item
        if axis == "mp":
            return (dp, flip(m, b))
        return (flip(dp, b), m)

    to_core = (dp, mc)
    to_x = (dp, mx)

    weights = [
        pltpu.make_async_copy(src, dst, w_sem.at[i])
        for i, (src, dst) in enumerate(
            [(wqkv_hbm, wqkv), (wout_hbm, wout), (wup_hbm, wup), (wdown_hbm, wdown)]
        )
    ]
    for w in weights:
        w.start()

    barrier = pltpu.get_barrier_semaphore()
    for item in bits:
        pl.semaphore_signal(barrier, inc=1, device_id=bit_partner(item), device_id_type=MESH)
    pl.semaphore_wait(barrier, len(bits))

    def small_copy(step, src, dst):
        return pltpu.make_async_remote_copy(
            src_ref=src, dst_ref=dst, send_sem=cnt_ss.at[step], recv_sem=cnt_rs.at[step],
            device_id=bit_partner(bits[step]), device_id_type=MESH,
        )

    cnt[0] = jnp.zeros((8, 128), F32) + jnp.sum(valid_ref[...])

    count_copies = []

    def count_send(step):
        cp = small_copy(step, cnt.at[step], cnt_r.at[step])
        cp.start()
        count_copies.append(cp)

    def count_next(step):
        count_copies[step].wait()
        cnt[step + 1] = cnt[step] + cnt_r[step]
        if step + 1 < len(bits):
            count_send(step + 1)

    count_send(0)

    def ag_copy(site, j, kind, ref, block, device):
        part = ref.at[block, pl.ds(j * rc, rc)]
        return pltpu.make_async_remote_copy(
            src_ref=part, dst_ref=part, send_sem=ag_ss.at[site, j, kind],
            recv_sem=ag_rs.at[site, j, kind], device_id=device, device_id_type=MESH,
        )

    def ag_start(site, j, ref, value):
        ref[m, pl.ds(j * rc, rc), :] = value
        cx = ag_copy(site, j, 0, ref, m, to_x)
        cx.start()
        cc = ag_copy(site, j, 1, ref, m, to_core)
        cc.start()
        return cx, cc

    def ag_forward(site, j, ref):
        cf = ag_copy(site, j, 2, ref, mx, to_core)
        cf.start()
        return cf

    def rs_copy(site, j, kind, src, dst, device):
        return pltpu.make_async_remote_copy(
            src_ref=src, dst_ref=dst, send_sem=rs_ss.at[site, j, kind],
            recv_sem=rs_rs.at[site, j, kind], device_id=device, device_id_type=MESH,
        )

    def rs_start(site, j, lhs_of, rhs_of):
        def product(first, slot):
            lhs = lhs_of(first)

            def tile_body(n, carry):
                lanes = pl.ds(pl.multiple_of(n * TILE, TILE), TILE)
                rhs, dims = rhs_of(lanes)
                tmp[slot, :, :, lanes] = mm(lhs, rhs, dims).reshape(2, rc, TILE)
                return carry

            lax.fori_loop(0, D // TILE, tile_body, 0)

        product(2 * (1 - chip), 0)
        rs_cs[j, 0] = tmp[0, 1 - core].astype(BF16)
        c0 = rs_copy(site, j, 0, rs_cs.at[j, 0], rs_cr.at[j, 0], to_core)
        c0.start()
        product(2 * chip, 1)
        rs_cs[j, 1] = tmp[1, 1 - core].astype(BF16)
        c1 = rs_copy(site, j, 1, rs_cs.at[j, 1], rs_cr.at[j, 1], to_core)
        c1.start()
        keep[j] = tmp[1, core]
        c0.wait()
        rs_xs[j] = (tmp[0, core] + rs_cr[j, 0].astype(F32)).astype(BF16)
        cx = rs_copy(site, j, 2, rs_xs.at[j], rs_xr.at[j], to_x)
        cx.start()
        return c1, cx

    def rs_finish(j, copies):
        for cp in copies:
            cp.wait()
        return keep[j] + rs_cr[j, 1].astype(F32) + rs_xr[j].astype(F32)

    vg_ref[...] = jnp.zeros(vg_ref.shape, F32)
    ag = {}
    for j in range(C):
        rows = slice(j * rc, (j + 1) * rc)
        normed, inverse = norm_rows(x_ref[rows, :].astype(F32))
        n1[rows, :] = normed
        inv1[rows, :] = inverse
        ag[j] = ag_start(0, j, g1, (normed * vec_ref[0:1, :] + vec_ref[1:2, :]).astype(BF16))

    head_lanes = pl.ds(pl.multiple_of(m * HW, HW), HW)
    weights[0].wait()

    def project(o):
        p = mm(g1[o], wqkv[...], NN)
        at = pl.ds(pl.multiple_of(o * R, R), R)
        q = (p[:, :HW] + vec_ref[6:7, head_lanes]).astype(BF16)
        k = p[:, HW : 2 * HW].astype(BF16)
        v = (p[:, 2 * HW :] + vec_ref[7:8, head_lanes]).astype(BF16)
        qkv[at, 0:HW] = q
        qkv[at, HW : 2 * HW] = k
        qkv[at, 2 * HW :] = v
        qT[:, at] = q.T
        kT[:, at] = k.T
        vT[:, at] = v.T

    project(m)
    count_next(0)
    for j in range(C):
        ag[j][1].wait()
    project(mc)
    count_next(1)
    fw = {}
    for j in range(C):
        ag[j][0].wait()
        fw[j] = ag_forward(0, j, g1)
    project(mx)
    for j in range(C):
        fw[j].wait()
    project(md)

    pair_row = lax.broadcasted_iota(jnp.int32, (2 * HD, BQ), 0) // HD
    pair_lane = lax.broadcasted_iota(jnp.int32, (BQ, 2 * HD), 1) // HD
    scale2 = log2_e / math.sqrt(HD)

    def make_dist(i, ke):
        key = lax.broadcasted_iota(jnp.int32, (ke, BQ), 0)
        query = lax.broadcasted_iota(jnp.int32, (ke, BQ), 1) + i * BQ
        apart = query - key
        allowed = (apart >= 0) & (segc_ref[0:ke, :] == segr_ref[:, i * BQ : (i + 1) * BQ])
        dist[0:ke, :] = jnp.where(allowed, apart.astype(F32), jnp.inf)

    def head_slope(h):
        head = jnp.zeros((1, BQ), jnp.int32) + (m * (HW // HD) + h + 1)
        return jnp.exp2(head.astype(F32) * (-8.0 / HEADS)) * log2_e

    def head_scores(i, ke, h):
        lanes = pl.ds(pl.multiple_of((h // 2) * 2 * HD, 2 * HD), 2 * HD)
        k_lanes = pl.ds(pl.multiple_of(HW + (h // 2) * 2 * HD, 2 * HD), 2 * HD)
        mask = (pair_row == lax.rem(h, 2)).astype(F32).astype(BF16)
        q_cols = qT[lanes, i * BQ : (i + 1) * BQ] * mask
        raw = mm(qkv[0:ke, k_lanes], q_cols, NN)
        return raw * scale2 - head_slope(h) * dist[0:ke, :]

    n_blocks = T // BQ
    for i in range(n_blocks):
        ke = (i + 1) * BQ
        make_dist(i, ke)

        def head_body(h, carry):
            s = head_scores(i, ke, h)
            top = jnp.max(s, 0, keepdims=True)
            e = jnp.exp2(s - top)
            total = jnp.sum(e, 0, keepdims=True)
            p = (e * (1.0 / total)).astype(BF16)
            lse[h, :, i * BQ : (i + 1) * BQ] = top + jnp.log2(total)
            at = pl.ds(pl.multiple_of(h * HD, HD), HD)
            mixT[at, i * BQ : (i + 1) * BQ] = mm(vT[at, 0:ke], p, NN).astype(BF16)
            return carry

        lax.fori_loop(0, HW // HD, head_body, 0)
        mix[i * BQ : (i + 1) * BQ, :] = mixT[:, i * BQ : (i + 1) * BQ].T
        if i < len(bits) - 2:
            count_next(i + 2)
    for step in range(2 + n_blocks, len(bits)):
        count_next(step)

    def rows4(ref, j):
        v = ref[:, pl.ds(j * rc, rc), :]
        return v.reshape(v.shape[0] * rc, v.shape[2])

    def pair_rows(ref, j):
        def of(first):
            v = ref[pl.ds(first, 2), pl.ds(j * rc, rc), :]
            return v.reshape(2 * rc, v.shape[2])

        return of

    def pair_mix(j):
        def of(first):
            a = mix[pl.ds(pl.multiple_of(first * R + j * rc, rc), rc), :]
            b = mix[pl.ds(pl.multiple_of(first * R + R + j * rc, rc), rc), :]
            return jnp.concatenate([a, b], 0)

        return of

    weights[1].wait()
    rs = {}
    for j in range(C):
        rs[j] = rs_start(0, j, pair_mix(j), lambda lanes: (wout[:, lanes], NN))
    for j in range(C):
        rows = slice(j * rc, (j + 1) * rc)
        hid = x_ref[rows, :].astype(F32) + rs_finish(j, rs[j]) + vec_ref[2:3, :]
        hidden[rows, :] = hid
        normed, inverse = norm_rows(hid)
        n2[rows, :] = normed
        inv2[rows, :] = inverse
        ag[j] = ag_start(1, j, g2, (normed * vec_ref[3:4, :] + vec_ref[4:5, :]).astype(BF16))

    def ag_finish(site, j, ref):
        ag[j][0].wait()
        cf = ag_forward(site, j, ref)
        ag[j][1].wait()
        cf.wait()

    weights[2].wait()
    weights[3].wait()
    for j in range(C):
        ag_finish(1, j, g2)
        rows = rows4(g2, j)

        def up_body(n, carry):
            lanes = pl.ds(pl.multiple_of(n * TILE, TILE), TILE)
            u = mm(rows, wup[:, lanes], NN) + vec_ref[pl.ds(8 + m, 1), lanes]
            a, b = gelu_both(u)
            act[:, pl.ds(j * rc, rc), lanes] = a.astype(BF16).reshape(mp_size, rc, TILE)
            gelub[:, pl.ds(j * rc, rc), lanes] = b.reshape(mp_size, rc, TILE)
            return carry

        lax.fori_loop(0, FU // TILE, up_body, 0)
        rs[j] = rs_start(1, j, pair_rows(act, j), lambda lanes: (wdown[:, lanes], NN))

    loss_scale = float(dp_size * mp_size * R) / cnt[len(bits), 0:1, 0:1]
    for j in range(C):
        rows = slice(j * rc, (j + 1) * rc)
        out = hidden[rows, :] + rs_finish(j, rs[j]) + vec_ref[5:6, :]
        bo_ref[rows, :] = out.astype(BF16)
        grad = valid_ref[rows, :] * (out - t_ref[rows, :].astype(F32)) * loss_scale
        go[rows, :] = grad
        ag[j] = ag_start(2, j, g3, grad.astype(BF16))
        vg_ref[5:6, :] += jnp.sum(grad, 0, keepdims=True)

    for j in range(C):
        ag_finish(2, j, g3)
        rows = rows4(g3, j)

        def act_body(n, carry):
            lanes = pl.ds(pl.multiple_of(n * TILE, TILE), TILE)
            ga = mm(rows, wdown[lanes, :], NT)
            gu = ga * gelub[:, pl.ds(j * rc, rc), lanes].reshape(mp_size * rc, TILE)
            gup[:, pl.ds(j * rc, rc), lanes] = gu.astype(BF16).reshape(mp_size, rc, TILE)
            return carry

        lax.fori_loop(0, FU // TILE, act_body, 0)
        rs[j] = rs_start(2, j, pair_rows(gup, j), lambda lanes: (wup[lanes, :], NT))

    def put_out(src, dst):
        cp = pltpu.make_async_copy(src, dst, stage_sem)
        cp.start()
        cp.wait()

    def down_body(n, carry):
        lanes = pl.ds(pl.multiple_of(n * TILE, TILE), TILE)
        left = act[:, :, lanes].reshape(T, TILE)
        stage[...] = mm(left, g3[...].reshape(T, D), TN)
        put_out(stage, ddown_hbm.at[lanes, :])
        return carry

    lax.fori_loop(0, FU // TILE, down_body, 0)

    for j in range(C):
        rows = slice(j * rc, (j + 1) * rc)
        gs = rs_finish(j, rs[j])
        gh = go[rows, :] + norm_backward(gs, n2[rows, :], inv2[rows, :], vec_ref[3:4, :])
        hidden[rows, :] = gh
        ag[j] = ag_start(3, j, g4, gh.astype(BF16))
        vg_ref[2:3, :] += jnp.sum(gh, 0, keepdims=True)
        vg_ref[3:4, :] += jnp.sum(gs * n2[rows, :], 0, keepdims=True)
        vg_ref[4:5, :] += jnp.sum(gs, 0, keepdims=True)

    def up_grad_body(n, carry):
        lanes = pl.ds(pl.multiple_of(n * TILE, TILE), TILE)
        left = g2[:, :, lanes].reshape(T, TILE)
        stage[...] = mm(left, gup[...].reshape(T, FU), TN)
        put_out(stage, dup_hbm.at[lanes, :])
        return carry

    lax.fori_loop(0, D // TILE, up_grad_body, 0)
    vg_ref[pl.ds(8 + m, 1), :] = jnp.sum(gup[...].reshape(T, FU).astype(F32), 0, keepdims=True)

    for j in range(C):
        ag_finish(3, j, g4)

    def gm_body(o, carry):
        at = pl.ds(pl.multiple_of(o * R, R), R)
        gmx = mm(g4[o], wout[...], NT).astype(BF16)
        gm[at, :] = gmx
        gmT[:, at] = gmx.T
        return carry

    lax.fori_loop(0, mp_size, gm_body, 0)

    gk[...] = jnp.zeros(gk.shape, F32)
    gv[...] = jnp.zeros(gv.shape, F32)
    for i in range(n_blocks):
        ke = (i + 1) * BQ
        block = slice(i * BQ, (i + 1) * BQ)
        make_dist(i, ke)

        def back_body(h, carry):
            lanes = pl.ds(pl.multiple_of((h // 2) * 2 * HD, 2 * HD), 2 * HD)
            v_lanes = pl.ds(pl.multiple_of(2 * HW + (h // 2) * 2 * HD, 2 * HD), 2 * HD)
            row_mask = (pair_row == lax.rem(h, 2)).astype(F32).astype(BF16)
            lane_mask = (pair_lane == lax.rem(h, 2)).astype(F32).astype(BF16)
            p = jnp.exp2(head_scores(i, ke, h) - lse[h, :, block])
            gp = mm(qkv[0:ke, v_lanes], gmT[lanes, block] * row_mask, NN)
            inner = jnp.sum(p * gp, 0, keepdims=True)
            raw = (p * (gp - inner)).astype(BF16)
            gv[0:ke, lanes] += mm(p.astype(BF16), gm[block, lanes] * lane_mask, NN)
            gk[0:ke, lanes] += mm(raw, qkv[block, lanes] * lane_mask, NN)
            at = pl.ds(pl.multiple_of(h * HD, HD), HD)
            gqT[at, block] = mm(kT[at, 0:ke], raw, NN) * (1.0 / math.sqrt(HD))
            return carry

        lax.fori_loop(0, HW // HD, back_body, 0)
        st[block, 0:HW] = gqT[:, block].T.astype(BF16)
    st[:, HW : 2 * HW] = (gk[...] * (1.0 / math.sqrt(HD))).astype(BF16)
    st[:, 2 * HW :] = gv[...].astype(BF16)
    vg_ref[6:7, head_lanes] = jnp.sum(st[:, 0:HW].astype(F32), 0, keepdims=True)
    vg_ref[7:8, head_lanes] = jnp.sum(st[:, 2 * HW :].astype(F32), 0, keepdims=True)

    def pair_st(j):
        def of(first):
            a = st[pl.ds(pl.multiple_of(first * R + j * rc, rc), rc), :]
            b = st[pl.ds(pl.multiple_of(first * R + R + j * rc, rc), rc), :]
            return jnp.concatenate([a, b], 0)

        return of

    for j in range(C):
        rs[j] = rs_start(3, j, pair_st(j), lambda lanes: (wqkv[lanes, :], NT))

    def out_grad_body(n, carry):
        lanes = pl.ds(pl.multiple_of(n * TILE, TILE), TILE)
        stage[...] = mm(mix[:, lanes], g4[...].reshape(T, D), TN)
        put_out(stage, dout_hbm.at[lanes, :])
        return carry

    lax.fori_loop(0, HW // TILE, out_grad_body, 0)

    def qkv_grad_body(n, carry):
        lanes = pl.ds(pl.multiple_of(n * TILE, TILE), TILE)
        left = g1[:, :, lanes].reshape(T, TILE)
        stage[:, 0 : 3 * HW] = mm(left, st[...], TN)
        put_out(stage.at[:, 0 : 3 * HW], dqkv_hbm.at[lanes, :])
        return carry

    lax.fori_loop(0, D // TILE, qkv_grad_body, 0)

    for j in range(C):
        rows = slice(j * rc, (j + 1) * rc)
        gf = rs_finish(j, rs[j])
        ig_ref[rows, :] = hidden[rows, :] + norm_backward(
            gf, n1[rows, :], inv1[rows, :], vec_ref[0:1, :]
        )
        vg_ref[0:1, :] += jnp.sum(gf * n1[rows, :], 0, keepdims=True)
        vg_ref[1:2, :] += jnp.sum(gf, 0, keepdims=True)


def block_call(sizes, x, teacher, segments, valid, vectors, wqkv, wout, wup, wdown):
    dp_size, mp_size = sizes
    R, D = x.shape
    T = mp_size * R
    HW = wout.shape[0]
    FU = wup.shape[1]
    C = CHUNKS
    rc = R // C
    n_bits = (dp_size * mp_size).bit_length() - 1
    vmem = pl.BlockSpec(memory_space=pltpu.VMEM)
    anywhere = pl.BlockSpec(memory_space=pl.ANY)
    dma = pltpu.SemaphoreType.DMA
    V = pltpu.VMEM
    scratch = [
        V((D, 3 * HW), BF16), V((HW, D), BF16), V((D, FU), BF16), V((FU, D), BF16), dma((4,)),
        V((mp_size, R, D), BF16), V((mp_size, R, D), BF16), V((mp_size, R, D), BF16), V((mp_size, R, D), BF16),
        V((T, 3 * HW), BF16), V((HW, T), BF16), V((HW, T), BF16), V((HW, T), BF16),
        V((HW, T), BF16), V((T, HW), BF16), V((HW // HD, 1, T), F32), V((T, BQ), F32),
        V((R, D), F32), V((R, D), F32), V((R, D), F32), V((R, 1), F32), V((R, 1), F32), V((R, D), F32),
        V((mp_size, R, FU), BF16), V((mp_size, R, FU), F32), V((mp_size, R, FU), BF16),
        V((T, HW), BF16), V((HW, T), BF16), V((T, HW), F32), V((T, HW), F32), V((HW, T), F32), V((T, 3 * HW), BF16),
        V((2, 2, rc, D), F32), V((C, rc, D), F32),
        V((C, 2, rc, D), BF16), V((C, 2, rc, D), BF16), V((C, rc, D), BF16), V((C, rc, D), BF16),
        V((n_bits + 1, 8, 128), F32), V((n_bits, 8, 128), F32), V((TILE, D), F32), dma,
        dma((4, C, 3)), dma((4, C, 3)), dma((4, C, 3)), dma((4, C, 3)), dma((n_bits,)), dma((n_bits,)),
    ]
    out_shape = [
        jax.ShapeDtypeStruct((R, D), BF16),
        jax.ShapeDtypeStruct((R, D), F32),
        jax.ShapeDtypeStruct((16, D), F32),
        jax.ShapeDtypeStruct((D, 3 * HW), F32),
        jax.ShapeDtypeStruct((HW, D), F32),
        jax.ShapeDtypeStruct((D, FU), F32),
        jax.ShapeDtypeStruct((FU, D), F32),
    ]
    return pl.pallas_call(
        functools.partial(block_kernel, sizes),
        out_shape=out_shape,
        in_specs=[vmem] * 6 + [anywhere] * 4,
        out_specs=[vmem] * 3 + [anywhere] * 4,
        scratch_shapes=scratch,
        compiler_params=pltpu.CompilerParams(
            collective_id=0, has_side_effects=True, vmem_limit_bytes=60 << 20
        ),
        name="block",
    )(
        x, teacher, segments.reshape(1, T), segments.reshape(T, 1),
        valid.reshape(R, 1), vectors, wqkv, wout, wup, wdown,
    )


def adam_update(gradient, stored, decay_factor, token_total):
    weight = stored[0]
    mean_grad = gradient / token_total
    moment_one = beta_one * stored[1] + (1.0 - beta_one) * mean_grad
    moment_two = beta_two * stored[2] + (1.0 - beta_two) * mean_grad * mean_grad
    update = (
        moment_one / correction_one / (jnp.sqrt(moment_two / correction_two) + adam_eps)
        + decay_factor * weight
    )
    weight = weight - learn_rate * update
    return (jnp.stack([weight, moment_one, moment_two]), weight.astype(jnp.bfloat16))


def shards(
    inputs,
    teacher,
    segments,
    valid_mask,
    qkv_copy,
    out_copy,
    up_copy,
    down_copy,
    vector_copy,
    qkv_state,
    out_state,
    up_state,
    down_state,
    vector_state,
):
    sizes = (lax.axis_size("dp"), lax.axis_size("mp"))
    token_total = inputs.shape[0] * sizes[0] * sizes[1]
    width = inputs.shape[1]
    head_width = qkv_copy.shape[2]
    block_out, input_grad, vector_local, qkv_local, out_local, up_local, down_local = block_call(
        sizes,
        inputs,
        teacher,
        segments,
        valid_mask.astype(F32),
        vector_copy.astype(F32),
        qkv_copy.reshape(width, 3 * head_width),
        out_copy,
        up_copy,
        down_copy,
    )
    qkv_local = qkv_local.reshape(width, 3, head_width)
    vector_grad = lax.psum(vector_local[: vector_copy.shape[0]], ("dp", "mp"))
    qkv_grad, out_grad, up_grad, down_grad = (
        lax.psum_scatter(qkv_local, "dp", scatter_dimension=0, tiled=True),
        lax.psum_scatter(out_local, "dp", scatter_dimension=1, tiled=True),
        lax.psum_scatter(up_local, "dp", scatter_dimension=0, tiled=True),
        lax.psum_scatter(down_local, "dp", scatter_dimension=1, tiled=True),
    )
    qkv_new, qkv_low = adam_update(qkv_grad, qkv_state, decay_rate, token_total)
    out_new, out_low = adam_update(out_grad, out_state, decay_rate, token_total)
    up_new, up_low = adam_update(up_grad, up_state, decay_rate, token_total)
    down_new, down_low = adam_update(down_grad, down_state, decay_rate, token_total)
    vector_new, vector_low = adam_update(vector_grad, vector_state, 0.0, token_total)
    qkv_full, out_full, up_full, down_full = (
        lax.all_gather(qkv_low, "dp", axis=0, tiled=True),
        lax.all_gather(out_low, "dp", axis=1, tiled=True),
        lax.all_gather(up_low, "dp", axis=0, tiled=True),
        lax.all_gather(down_low, "dp", axis=1, tiled=True),
    )
    return (
        block_out,
        input_grad,
        qkv_grad,
        out_grad,
        up_grad,
        down_grad,
        vector_grad,
        qkv_new,
        out_new,
        up_new,
        down_new,
        vector_new,
        qkv_full,
        out_full,
        up_full,
        down_full,
        vector_low,
    )


def solution(mesh):
    in_specs = (
        P(("dp", "mp"), None),
        P(("dp", "mp"), None),
        P("dp", None),
        P(("dp", "mp")),
        P(None, None, "mp"),
        P("mp", None),
        P(None, "mp"),
        P("mp", None),
        P(),
        P(None, "dp", None, "mp"),
        P(None, "mp", "dp"),
        P(None, "dp", "mp"),
        P(None, "mp", "dp"),
        P(),
    )
    out_specs = (
        P(("dp", "mp"), None),
        P(("dp", "mp"), None),
        P("dp", None, "mp"),
        P("mp", "dp"),
        P("dp", "mp"),
        P("mp", "dp"),
        P(),
        P(None, "dp", None, "mp"),
        P(None, "mp", "dp"),
        P(None, "dp", "mp"),
        P(None, "mp", "dp"),
        P(),
        P(None, None, "mp"),
        P("mp", None),
        P(None, "mp"),
        P("mp", None),
        P(),
    )
    return jax.shard_map(shards, mesh=mesh, in_specs=in_specs, out_specs=out_specs, check_vma=False)
```

time: 874 us -> 658 us (0.75)
  matrix products: 150 us -> 0 us
  Pallas kernels: 0 us -> 149 us
  waiting for transfers between devices: 484 us -> 385 us
  other arithmetic: 58.6 us -> 16.3 us
  blocking collectives: 107 us -> 70.3 us
  local copies, waits for them, and re-layouts: 37.6 us -> 21.7 us
  starting transfers between devices: 12.2 us -> 0.28 us
    dot_general x26 -> x0, matrix products: 150 us -> none  [the longest x2 27.8 us: one_block(): jnp.einsum('hqk,qhd->khd', grad_raw, block_query, preferred_element_type=...]
    pallas_call x0 -> x1, Pallas kernels: none -> 149 us  [block_call(): pl.pallas_call(functools.partial(block_kernel, sizes), out_shape=out_shap...]
    reduce_scatter x4 -> x0, waiting for transfers between devices: 108 us -> none  [the longest x1 44.6 us: shards(): lax.psum_scatter(jnp.einsum('rf,df->rd', grad_up, up_copy, preferred_elem...]
    reduce_scatter x1, waiting for transfers between devices: 0.02 us -> 90.6 us  [shards(): lax.psum_scatter(down_local, 'dp', scatter_dimension=1, tiled=True)]
    all_gather x4 -> x0, waiting for transfers between devices: 65.1 us -> none  [the longest x1 23.3 us: shards(): lax.all_gather(norm_one.astype(jnp.bfloat16), 'mp', axis=0, tiled=True)]
    reduce_scatter x1, waiting for transfers between devices: 66.7 us -> 22.5 us  [shards(): lax.psum_scatter(out_local, 'dp', scatter_dimension=1, tiled=True)]
    psum x2 -> x1, blocking collectives: 80.1 us -> 40.8 us  [shards(): vector_grad = lax.psum(vector_local[:vector_copy.shape[0]], ('dp', 'mp'))]
    reduce_sum x13 -> x0, other arithmetic: 21.2 us -> none  [the longest x2 5.94 us: one_block(): row_total = jnp.sum(exponent, -1, keepdims=True)]
  transfers between devices with their start and end apart: 15 -> 7, of which waited for: 13 -> 7; matrix products, arithmetic and copies ran while one was open for 17% -> 3% of each run, Pallas kernels for 0% -> 0%
where the time goes in v1:
time: 658 us
  waiting for transfers between devices  385 us (59%)
  Pallas kernels  149 us (23%)
  blocking collectives  70.3 us (11%)
  local copies, waits for them, and re-layouts  21.7 us (3%)
  other arithmetic  16.3 us (2%)
  between operations  14.3 us (2%)
    pallas_call x1, Pallas kernels, block_call(): pl.pallas_call(functools.partial(block_kernel, sizes), out_shape=out_shap...  149 us
    reduce_scatter x1, waiting for transfers between devices, shards(): lax.psum_scatter(down_local, 'dp', scatter_dimension=1, tiled=True)  90.6 us
    reduce_scatter x1, waiting for transfers between devices, shards(): lax.psum_scatter(up_local, 'dp', scatter_dimension=0, tiled=True)  88.9 us
    reduce_scatter x1, waiting for transfers between devices, shards(): lax.psum_scatter(qkv_local, 'dp', scatter_dimension=0, tiled=True)  71 us
    all_gather x1, waiting for transfers between devices, shards(): lax.all_gather(down_low, 'dp', axis=1, tiled=True)  52.4 us
    all_gather x1, waiting for transfers between devices, shards(): lax.all_gather(up_low, 'dp', axis=0, tiled=True)  47.7 us
    psum x1, blocking collectives, shards(): vector_grad = lax.psum(vector_local[:vector_copy.shape[0]], ('dp', 'mp'))  40.8 us
    all_gather x1, blocking collectives, shards(): lax.all_gather(out_low, 'dp', axis=1, tiled=True)  29.5 us
  transfers between devices with their start and end apart: 7, of which 7 were waited for; matrix products, arithmetic and copies ran while one was open for 3% of the time, Pallas kernels for 0%

profile of v1, /device:TPU:0, one launch (start us, length us, event | category | flops | bytes accessed | tf_op | source)
XLA Modules:
  0.0 657.7 jit_solution(1786720740828185259)
XLA Ops:
  7.2 1.7 copy.33
  9.0 1.6 copy.36.wqkv_hbm
  10.6 1.0 copy.34.segc_ref
  11.6 0.8 copy.35.valid_ref
  12.4 0.6 convert_element_type.22.vec_ref
  13.0 149.5 %block.1 = (bf16[256,1024]{1,0:T(8,128)(2,1)}, f32[256,1024]{1,0:T(8,128)}, f32[16,1024]{1,0:T(8,128)}, f32[1024,768]{1,0:T(8,128)}, f32[256,1024]{1,0:T(8,128)}...) custom-call(bf16[256,1024]{1,0:T(8,128)(2,1)} %x_ref.1, bf16[256,1024]{1,0:T(8,128)(2,1)} %t_ref.1, s32[1,1024]{1,0:T(1,128)} %segr_ref.1, ...), custom_call_target="tpu_custom_call" | custom-call | tf_op jit(solution)/shard_map/block/pallas_call | solution.py:518
  162.5 3.6 copy.37
  166.1 0.0 reduce-scatter.9.cloned.1.call-start
  166.2 0.7 reduce-scatter.9.cloned.1.call-update
  166.9 0.0 reduce-scatter.11.cloned.1.call-start
  167.0 0.7 reduce-scatter.11.cloned.1.call-update
  167.7 0.5 reduce-scatter.7.cloned.1.call-update
  168.2 0.0 all-gather.4.cloned.1.call-start
  168.3 0.1 fusion.25
  168.3 0.2 copy.44
  168.5 0.2 copy.45
  168.7 0.2 copy.46
  168.9 71.0 %reduce-scatter.5.cloned.1.call-done = f32[128,3,256]{0,2,1:T(8,128)} async-done(((f32[1024,3,256]{0,2,1:T(8,128)}), f32[128,3,256]{0,2,1:T(8,128)}) %reduce-scatter.5.cloned.1.call-update) | async-done | bytes 393232 | tf_op jit(solution)/shard_map/reduce_scatter | solution.py:582
  239.9 2.4 fusion.24
  242.3 0.0 all-gather.6.cloned.1.call-start
  242.4 88.9 %reduce-scatter.9.cloned.1.call-done = f32[128,1024]{1,0:T(8,128)} async-done(((f32[1024,1024]{1,0:T(8,128)}), f32[128,1024]{1,0:T(8,128)}) %reduce-scatter.9.cloned.1.call-update) | async-done | bytes 524304 | tf_op jit(solution)/shard_map/reduce_scatter | solution.py:584
  331.2 2.2 fusion.22
  333.5 0.0 all-gather.8.cloned.1.call-start
  333.5 90.6 %reduce-scatter.11.cloned.1.call-done = f32[1024,128]{1,0:T(8,128)} async-done(((f32[1024,1024]{1,0:T(8,128)}), f32[1024,128]{1,0:T(8,128)}) %reduce-scatter.11.cloned.1.call-update) | async-done | bytes 524304 | tf_op jit(solution)/shard_map/reduce_scatter | solution.py:585
  424.1 2.9 fusion.21
  427.0 40.8 %psum.7 = f32[12,1024]{1,0:T(8,128)S(1)} all-reduce(f32[12,1024]{1,0:T(8,128)S(1)} %bitcast.157), channel_id=1, replica_groups=mesh['dp'=8,'mp'=4] {'dp','mp'}, use_global_device_ids=true, to_apply=%region_4.0 | all-reduce | flops 12288 | bytes 98304 | tf_op jit(solution)/shard_map/psum | solution.py:580
  467.8 0.7 fusion.20
  468.5 0.7 pad_maximum_fusion.4
  469.2 22.5 %reduce-scatter.7.cloned.1.call-done = f32[256,128]{1,0:T(8,128)} async-done(((f32[256,1024]{1,0:T(8,128)}), f32[256,128]{1,0:T(8,128)}) %reduce-scatter.7.cloned.1.call-update) | async-done | bytes 131088 | tf_op jit(solution)/shard_map/reduce_scatter | solution.py:583
  491.7 1.0 fusion.23
  492.7 29.5 %all_gather.13 = bf16[256,1024]{1,0:T(8,128)(2,1)} all-gather(bf16[256,128]{1,0:T(8,128)(2,1)S(1)} %get-tuple-element.54), channel_id=1, replica_groups=mesh['dp'=8,'mp'=4] {'dp'}, dimensions={1}, use_global_device_ids=true | all-gather | bytes 589824 | tf_op jit(solution)/shard_map/all_gather | solution.py:594
  522.2 0.8 pad_maximum_fusion.3
  523.0 1.4 pad_maximum_fusion.2
  524.4 1.4 copy.42
  525.8 1.9 copy.41
  527.7 2.4 pad_maximum_fusion.1
  530.1 1.2 pad_maximum_fusion
  531.4 10.3 %all-gather.4.cloned.1.call-done = bf16[1024,3,256]{0,2,1:T(8,128)(2,1)} async-done(((bf16[128,3,256]{0,2,1:T(8,128)(2,1)}), bf16[1024,3,256]{0,2,1:T(8,128)(2,1)}) %all-gather.4.cloned.1.call-update) | async-done | bytes 1572880 | tf_op jit(solution)/shard_map/all_gather | solution.py:593
  541.7 2.6 copy.43
  544.2 47.7 %all-gather.6.cloned.1.call-done = bf16[1024,1024]{1,0:T(8,128)(2,1)} async-done(((bf16[128,1024]{1,0:T(8,128)(2,1)}), bf16[1024,1024]{1,0:T(8,128)(2,1)}) %all-gather.6.cloned.1.call-update) | async-done | bytes 2097168 | tf_op jit(solution)/shard_map/all_gather | solution.py:595
  592.0 52.4 %all-gather.8.cloned.1.call-done = bf16[1024,1024]{1,0:T(8,128)(2,1)} async-done(((bf16[1024,128]{1,0:T(8,128)(2,1)}), bf16[1024,1024]{1,0:T(8,128)(2,1)}) %all-gather.8.cloned.1.call-update) | async-done | bytes 2097168 | tf_op jit(solution)/shard_map/all_gather | solution.py:596
  644.4 0.8 copy.52
  645.2 1.0 copy.53
  646.1 0.8 copy.54
  646.9 0.3 copy-done
  647.2 1.3 copy.55
  648.5 1.0 copy-done.1
  649.6 1.3 copy.56
  (33 shorter events, 0.2 us)
Async XLA Ops:
  7.2 232.7 %reduce-scatter.5.cloned.1.call-start = ((), (), s32[]{:S(2)}) async-start(), calls=%async_computation.4 | async-start | bytes 3538944 | tf_op jit(solution)/shard_map/reduce_scatter | solution.py:582
  9.0 1.6 copy-start.12
  9.0 2.6 copy-start.13
  9.0 3.4 copy-start.11
  166.1 165.1 %reduce-scatter.9.cloned.1.call-start = ((), (), s32[]{:S(2)}) async-start(), calls=%async_computation.6 | async-start | bytes 4718592 | tf_op jit(solution)/shard_map/reduce_scatter | solution.py:584
  166.9 257.2 %reduce-scatter.11.cloned.1.call-start = ((), (), s32[]{:S(2)}) async-start(), calls=%async_computation.7 | async-start | bytes 4718592 | tf_op jit(solution)/shard_map/reduce_scatter | solution.py:585
  166.9 1.3 copy-start.4
  167.6 324.1 %reduce-scatter.7.cloned.1.call-start = ((), (), s32[]{:S(2)}) async-start(), calls=%async_computation.5 | async-start | bytes 1179648 | tf_op jit(solution)/shard_map/reduce_scatter | solution.py:583
  168.2 373.5 %all-gather.4.cloned.1.call-start = ((), (), s32[]{:S(2)}) async-start(), calls=%async_computation.8 | async-start | bytes 1769472 | tf_op jit(solution)/shard_map/all_gather | solution.py:593
  168.8 162.4 %copy-start.3 = (f32[3,128,1024]{2,1,0:T(8,128)S(1)}, f32[3,128,1024]{2,1,0:T(8,128)}, u32[]{:S(2)}) copy-start(f32[3,128,1024]{2,1,0:T(8,128)} %param.25) | copy-start | bytes 4718596
  242.3 349.6 %all-gather.6.cloned.1.call-start = ((), (), s32[]{:S(2)}) async-start(), calls=%async_computation.9 | async-start | bytes 2359296 | tf_op jit(solution)/shard_map/all_gather | solution.py:595
  333.4 93.6 %copy-start.10 = (f32[16,1024]{1,0:T(8,128)S(1)}, f32[16,1024]{1,0:T(8,128)}, u32[]{:S(2)}) copy-start(f32[16,1024]{1,0:T(8,128)} %get-tuple-element.30) | copy-start | bytes 196612
  333.4 134.4 %copy-start.9 = (f32[3,12,1024]{2,1,0:T(8,128)S(1)}, f32[3,12,1024]{2,1,0:T(8,128)}, u32[]{:S(2)}) copy-start(f32[3,12,1024]{2,1,0:T(8,128)} %param.27) | copy-start | bytes 442372
  333.4 158.3 %copy-start.7 = (f32[3,256,128]{2,1,0:T(8,128)S(1)}, f32[3,256,128]{2,1,0:T(8,128)}, u32[]{:S(2)}) copy-start(f32[3,256,128]{2,1,0:T(8,128)} %param.24) | copy-start | bytes 1179652
  333.5 310.9 %all-gather.8.cloned.1.call-start = ((), (), s32[]{:S(2)}) async-start(), calls=%async_computation.10 | async-start | bytes 2359296 | tf_op jit(solution)/shard_map/all_gather | solution.py:596
  467.8 55.2 %copy-start.8 = (f32[12,1024]{1,0:T(8,128)}, f32[12,1024]{1,0:T(8,128)S(1)}, u32[]{:S(2)}) copy-start(f32[12,1024]{1,0:T(8,128)S(1)} %psum.7) | copy-start | bytes 147460
  531.4 113.0 %copy-start.6 = (bf16[256,1024]{1,0:T(8,128)(2,1)S(1)}, bf16[256,1024]{1,0:T(8,128)(2,1)}, u32[]{:S(2)}) copy-start(bf16[256,1024]{1,0:T(8,128)(2,1)} %get-tuple-element.88) | copy-start | bytes 1572868
  531.4 113.8 %copy-start.5 = (f32[256,1024]{1,0:T(8,128)S(1)}, f32[256,1024]{1,0:T(8,128)}, u32[]{:S(2)}) copy-start(f32[256,1024]{1,0:T(8,128)} %get-tuple-element.89) | copy-start | bytes 3145732
  644.4 1.8 copy-start.2
  645.2 2.1 copy-start
  647.2 2.3 copy-start.1
Sparse Core Ops, SparseCore 0:
  166.3 73.5 reduce-scatter.4
  244.1 87.0 reduce-scatter.8
  335.9 88.1 reduce-scatter.10
  427.9 63.7 reduce-scatter.6
  494.4 47.2 all-gather.3
  544.4 47.4 all-gather.5
  594.8 49.5 all-gather.7

commit v2 on v1

v2 whole, which is shorter than its diff:
```python
import functools
import math
import types

import jax
import jax.numpy as jnp
from jax import lax
from jax.experimental import pallas as pl
from jax.experimental.pallas import tpu as pltpu
from jax.sharding import PartitionSpec as P

HEADS = 16
HD = 64

norm_eps = 1e-05
beta_one = 0.9
beta_two = 0.95
adam_eps = 1e-08
learn_rate = 0.001
decay_rate = 0.1
correction_one = 1.0 - (0.9**10) ** 10
correction_two = 1.0 - (0.95**10) ** 10
log2_e = 1.4426950408889634

CHUNKS = 2
BQ = 256
TILE = 256
MESH = pl.DeviceIdType.MESH
F32 = jnp.float32
BF16 = jnp.bfloat16
NN = ((1,), (0,))
NT = ((1,), (1,))
TN = ((0,), (0,))


def mm(a, b, dims):
    return lax.dot_general(a, b, (dims, ((), ())), preferred_element_type=F32)


def gelu_both(v):
    c = 0.7978845608
    v2 = v * v
    th = jnp.tanh(c * (v + 0.044715 * v2 * v))
    half = 0.5 * (1.0 + th)
    back = half + 0.5 * v * (1.0 - th * th) * (c * (1.0 + 3.0 * 0.044715 * v2))
    return v * half, back


def norm_rows(v):
    centred = v - jnp.mean(v, -1, keepdims=True)
    inverse = lax.rsqrt(jnp.mean(centred * centred, -1, keepdims=True) + norm_eps)
    return centred * inverse, inverse


def norm_backward(grad_out, normed, inverse, gain_row):
    scaled = grad_out * gain_row
    return inverse * (
        scaled
        - jnp.mean(scaled, -1, keepdims=True)
        - normed * jnp.mean(scaled * normed, -1, keepdims=True)
    )


def adam_step(gradient, weight, first, second, decay_factor, token_total):
    mean_grad = gradient / token_total
    moment_one = beta_one * first + (1.0 - beta_one) * mean_grad
    moment_two = beta_two * second + (1.0 - beta_two) * mean_grad * mean_grad
    update = (
        moment_one / correction_one / (jnp.sqrt(moment_two / correction_two) + adam_eps)
        + decay_factor * weight
    )
    return weight - learn_rate * update, moment_one, moment_two


def block_kernel(sizes, fast, names, *refs):
    r = types.SimpleNamespace(**dict(zip(names, refs)))
    dp_size, mp_size = sizes
    dp = lax.axis_index("dp")
    m = lax.axis_index("mp")
    core = lax.rem(m, 2)
    chip = m // 2
    mc = m + 1 - 2 * core
    mx = lax.rem(m + 2, 4)
    md = mc + mx - m
    C = CHUNKS
    R, D = r.x.shape
    rc = R // C
    T = mp_size * R
    HW = r.wout.shape[0]
    FU = r.wup.shape[1]
    LOCAL_HEADS = HW // HD
    token_total = float(dp_size * T)

    bits = [("mp", b) for b in range(mp_size.bit_length() - 1)]
    bits += [("dp", b) for b in range(dp_size.bit_length() - 1)]

    def flip(v, b):
        w = 1 << b
        return v + w - 2 * w * lax.rem(v // w, 2)

    def bit_partner(item):
        axis, b = item
        if axis == "mp":
            return (dp, flip(m, b))
        return (flip(dp, b), m)

    to_core = (dp, mc)
    to_x = (dp, mx)

    NZ = dp_size // 2
    z = dp // 2
    y = lax.rem(dp, 2)
    to_y = (dp + 1 - 2 * y, m)

    def line(direction):
        place = z + direction * (NZ - 1 - 2 * z)
        return place, (dp + 2 - 4 * direction, m)

    def local_copy(src, dst, sem):
        cp = pltpu.make_async_copy(src, dst, sem)
        cp.start()
        return cp

    weights = [
        local_copy(src, dst, r.w_sem.at[i])
        for i, (src, dst) in enumerate(
            [(r.wqkv_hbm, r.wqkv), (r.wout_hbm, r.wout), (r.wup_hbm, r.wup), (r.wdown_hbm, r.wdown)]
        )
    ]
    if fast:
        parts = {
            "d": (0, r.g3, r.act, FU, True),
            "u": (1, r.g2, r.gup, FU, False),
            "o": (2, r.g4, r.mix, HW, True),
            "q": (3, r.g1, r.st, 3 * HW, False),
        }
        states = {
            "d": r.sd,
            "u": r.big.at[0:3, 0:SHARE, :],
            "o": r.so,
            "q": r.big.at[0:3, SHARE : 2 * SHARE, 0 : 3 * HW],
        }
        state_in = {}

        def fetch_state(name):
            state_in[name] = local_copy(
                getattr(r, "s%s_hbm" % name), states[name], r.s_sem.at[parts[name][0]]
            )

        fetch_state("d")
        fetch_state("o")

    barrier = pltpu.get_barrier_semaphore()
    for item in bits:
        pl.semaphore_signal(barrier, inc=1, device_id=bit_partner(item), device_id_type=MESH)
    greetings = len(bits)
    if fast:
        for direction in range(2):
            place, following = line(direction)

            @pl.when(place < NZ - 1)
            def _():
                pl.semaphore_signal(barrier, inc=1, device_id=following, device_id_type=MESH)

        greetings = greetings + (z > 0).astype(jnp.int32) + (z < NZ - 1).astype(jnp.int32)
    pl.semaphore_wait(barrier, greetings)

    def doubling(values, received, send_sems, recv_sems):
        copies = []

        def send(step):
            cp = pltpu.make_async_remote_copy(
                src_ref=values.at[step], dst_ref=received.at[step],
                send_sem=send_sems.at[step], recv_sem=recv_sems.at[step],
                device_id=bit_partner(bits[step]), device_id_type=MESH,
            )
            cp.start()
            copies.append(cp)

        def following():
            step = len(copies) - 1
            copies[step].wait()
            values[step + 1] = values[step] + received[step]
            if step + 1 < len(bits):
                send(step + 1)

        return send, following

    count_send, count_next = doubling(r.cnt, r.cnt_r, r.cnt_ss, r.cnt_rs)
    r.cnt[0] = jnp.zeros((8, 128), F32) + jnp.sum(r.valid[...])
    count_send(0)

    def ag_copy(site, j, kind, ref, block, device):
        part = ref.at[block, pl.ds(j * rc, rc)]
        return pltpu.make_async_remote_copy(
            src_ref=part, dst_ref=part, send_sem=r.ag_ss.at[site, j, kind],
            recv_sem=r.ag_rs.at[site, j, kind], device_id=device, device_id_type=MESH,
        )

    def ag_start(site, j, ref, value):
        ref[m, pl.ds(j * rc, rc), :] = value
        cx = ag_copy(site, j, 0, ref, m, to_x)
        cx.start()
        cc = ag_copy(site, j, 1, ref, m, to_core)
        cc.start()
        return cx, cc

    def ag_forward(site, j, ref):
        cf = ag_copy(site, j, 2, ref, mx, to_core)
        cf.start()
        return cf

    def rs_copy(site, j, kind, src, dst, device):
        return pltpu.make_async_remote_copy(
            src_ref=src, dst_ref=dst, send_sem=r.rs_ss.at[site, j, kind],
            recv_sem=r.rs_rs.at[site, j, kind], device_id=device, device_id_type=MESH,
        )

    def rs_start(site, j, lhs_of, rhs_of):
        def product(first, slot, kept_ref):
            lhs = lhs_of(first)

            def tile_body(n, carry):
                lanes = pl.ds(pl.multiple_of(n * TILE, TILE), TILE)
                rhs, dims = rhs_of(lanes)
                both = mm(lhs, rhs, dims)
                low, high = both[:rc], both[rc:]
                r.rs_cs[j, slot, :, lanes] = jnp.where(core == 0, high, low).astype(BF16)
                kept_ref[j, :, lanes] = jnp.where(core == 0, low, high)
                return carry

            lax.fori_loop(0, D // TILE, tile_body, 0)

        product(2 * (1 - chip), 0, r.pass_on)
        c0 = rs_copy(site, j, 0, r.rs_cs.at[j, 0], r.rs_cr.at[j, 0], to_core)
        c0.start()
        product(2 * chip, 1, r.keep)
        c1 = rs_copy(site, j, 1, r.rs_cs.at[j, 1], r.rs_cr.at[j, 1], to_core)
        c1.start()
        c0.wait()
        r.rs_xs[j] = (r.pass_on[j] + r.rs_cr[j, 0].astype(F32)).astype(BF16)
        cx = rs_copy(site, j, 2, r.rs_xs.at[j], r.rs_xr.at[j], to_x)
        cx.start()
        return c1, cx

    def rs_finish(j, copies):
        for cp in copies:
            cp.wait()
        return r.keep[j] + r.rs_cr[j, 1].astype(F32) + r.rs_xr[j].astype(F32)

    def share_rows(ref, share):
        lanes = pl.ds(pl.multiple_of(share * SHARE, SHARE), SHARE)
        return ref[:, :, lanes].reshape(T, SHARE).T

    def right_tile(ref, lanes):
        if len(ref.shape) == 3:
            return ref[:, :, lanes].reshape(T, TILE)
        return ref[:, lanes]

    def y_copy(name, i):
        p = parts[name][0]
        return pltpu.make_async_remote_copy(
            src_ref=getattr(r, "ys" + name).at[i], dst_ref=getattr(r, "yr" + name).at[i],
            send_sem=r.y_ss.at[p, i], recv_sem=r.y_rs.at[p, i], device_id=to_y, device_id_type=MESH,
        )

    def y_start(name):
        _, left, right, width, _ = parts[name]
        out = getattr(r, "ys" + name)

        def pair_body(i, carry):
            lhs = jnp.concatenate(
                [share_rows(left, 4 * i + 1 - y), share_rows(left, 4 * i + 3 - y)], 0
            )

            def tile_body(n, inner):
                lanes = pl.ds(pl.multiple_of(n * TILE, TILE), TILE)
                both = mm(lhs, right_tile(right, lanes), NN).astype(BF16)
                out[2 * i, :, lanes] = both[:SHARE]
                out[2 * i + 1, :, lanes] = both[SHARE:]
                return inner

            lax.fori_loop(0, width // TILE, tile_body, 0)
            y_copy(name, 2 * i).start()
            y_copy(name, 2 * i + 1).start()
            return carry

        lax.fori_loop(0, NZ // 2, pair_body, 0)

    def share_sum(name, target, put):
        _, left, right, width, _ = parts[name]
        got = getattr(r, "yr" + name)
        y_copy(name, target).wait_recv()
        lhs = share_rows(left, 2 * target + y)

        def tile_body(n, carry):
            lanes = pl.ds(pl.multiple_of(n * TILE, TILE), TILE)
            put(lanes, mm(lhs, right_tile(right, lanes), NN) + got[target, :, lanes].astype(F32))
            return carry

        lax.fori_loop(0, width // TILE, tile_body, 0)

    def z_copy(name, direction, step, device):
        p = parts[name][0]
        return pltpu.make_async_remote_copy(
            src_ref=getattr(r, "zs" + name).at[direction],
            dst_ref=getattr(r, "zr" + name).at[direction, step],
            send_sem=r.z_ss.at[p, direction, step], recv_sem=r.z_rs.at[p, direction, step],
            device_id=device, device_id_type=MESH,
        )

    def chain_step(name, step):
        out = getattr(r, "zs" + name)
        got = getattr(r, "zr" + name)

        def one(direction, carry):
            place, following = line(direction)

            @pl.when(place <= step)
            def _():
                mirrored = NZ - 1 - step + place
                target = mirrored + direction * (NZ - 1 - 2 * mirrored)

                def put(lanes, value):
                    r.acc[:, lanes] = value

                share_sum(name, target, put)
                if step > 0:

                    @pl.when(place < step)
                    def _():
                        z_copy(name, direction, step - 1, following).wait_send()

                    @pl.when(place > 0)
                    def _():
                        z_copy(name, direction, step - 1, following).wait_recv()
                        r.acc[:, 0 : out.shape[2]] += got[direction, step - 1].astype(F32)

                out[direction] = r.acc[:, 0 : out.shape[2]].astype(BF16)
                z_copy(name, direction, step, following).start()

            return carry

        lax.fori_loop(0, 2, one, 0)

    gathered = {}

    def a_src(name, share):
        ref = getattr(r, name + "_full")
        at = pl.ds(pl.multiple_of(share * SHARE, SHARE), SHARE)
        if parts[name][4]:
            return ref.at[:, at]
        return ref.at[at, :]

    def az_copy(name, direction, step, share, src, device):
        p = parts[name][0]
        return pltpu.make_async_remote_copy(
            src_ref=src, dst_ref=a_src(name, share), send_sem=r.az_ss.at[p, direction, step],
            recv_sem=r.az_rs.at[p, direction, step], device_id=device, device_id_type=MESH,
        )

    def ay_copy(name, place, src):
        p = parts[name][0]
        return pltpu.make_async_remote_copy(
            src_ref=src, dst_ref=a_src(name, 2 * place + y), send_sem=r.ay_ss.at[p, place],
            recv_sem=r.ay_rs.at[p, place], device_id=to_y, device_id_type=MESH,
        )

    local_out = []

    def finish_share(name):
        p, _, _, width, turned = parts[name]
        got = getattr(r, "zr" + name)
        state = states[name]
        grad_out = getattr(r, "gr" + name)
        fresh = getattr(r, "nc" + name)

        def put(lanes, value):
            r.acc[:, lanes] = value

        share_sum(name, z, put)

        def one(direction, carry):
            place, _ = line(direction)

            @pl.when(place > 0)
            def _():
                z_copy(name, direction, NZ - 2, (dp, m)).wait_recv()
                r.acc[:, 0:width] += got[direction, NZ - 2].astype(F32)

            return carry

        lax.fori_loop(0, 2, one, 0)
        state_in[name].wait()

        def adam_body(n, carry):
            cols = pl.ds(pl.multiple_of(n * SHARE, SHARE), SHARE)
            grad = r.acc[:, cols]
            if turned:
                grad = grad.T
                at = (cols, slice(None))
            else:
                at = (slice(None), cols)
            grad_out[at] = grad
            w, a, b = adam_step(
                grad, state[(0,) + at], state[(1,) + at], state[(2,) + at], decay_rate, token_total
            )
            state[(0,) + at] = w
            state[(1,) + at] = a
            state[(2,) + at] = b
            fresh[at] = w.astype(BF16)
            return carry

        lax.fori_loop(0, width // SHARE, adam_body, 0)
        for direction in range(2):
            place, following = line(direction)

            @pl.when(place < NZ - 1)
            def _():
                az_copy(name, direction, 0, 2 * z + y, fresh, following).start()

        ay_copy(name, z, fresh).start()
        local_out.append(local_copy(fresh, a_src(name, 2 * z + y), r.o_sem.at[p, 0]))
        local_out.append(local_copy(grad_out, getattr(r, name + "_grad"), r.o_sem.at[p, 1]))
        local_out.append(local_copy(state, getattr(r, name + "_new"), r.o_sem.at[p, 2]))

    def gather_step(name, step):
        for direction in range(2):
            place, following = line(direction)

            @pl.when(place >= step)
            def _():
                source = z - step + 2 * step * direction
                part = a_src(name, 2 * source + y)
                az_copy(name, direction, step - 1, 2 * source + y, part, following).wait_recv()
                if step < NZ - 1:

                    @pl.when(place < NZ - 1)
                    def _():
                        az_copy(name, direction, step, 2 * source + y, part, following).start()

                ay_copy(name, source, part).start()

    def gather_end(name):
        def one(direction, carry):
            place, following = line(direction)
            part = a_src(name, 2 * z + y)

            @pl.when(place <= NZ - 2)
            def _():
                z_copy(name, direction, NZ - 2, following).wait_send()

            for step in range(NZ - 1):

                @pl.when((place >= step) & (place < NZ - 1))
                def _():
                    az_copy(name, direction, step, 2 * z + y, part, following).wait_send()

            return carry

        lax.fori_loop(0, 2, one, 0)

        def y_body(i, carry):
            y_copy(name, i).wait_send()
            part = a_src(name, 2 * i + y)
            ay_copy(name, i, part).wait_send()
            ay_copy(name, i, part).wait_recv()
            return carry

        lax.fori_loop(0, NZ, y_body, 0)

    def put_out(src, dst):
        cp = pltpu.make_async_copy(src, dst, r.stage_sem)
        cp.start()
        cp.wait()

    r.vg[...] = jnp.zeros(r.vg.shape, F32)
    ag = {}
    for j in range(C):
        rows = slice(j * rc, (j + 1) * rc)
        normed, inverse = norm_rows(r.x[rows, :].astype(F32))
        ag[j] = ag_start(0, j, r.g1, (normed * r.vec[0:1, :] + r.vec[1:2, :]).astype(BF16))

    head_lanes = pl.ds(pl.multiple_of(m * HW, HW), HW)
    weights[0].wait()

    def project(o):
        p = mm(r.g1[o], r.wqkv[...], NN)
        at = pl.ds(pl.multiple_of(o * R, R), R)
        q = (p[:, :HW] + r.vec[6:7, head_lanes]).astype(BF16)
        k = p[:, HW : 2 * HW].astype(BF16)
        v = (p[:, 2 * HW :] + r.vec[7:8, head_lanes]).astype(BF16)
        r.qkv[at, 0:HW] = q
        r.qkv[at, HW : 2 * HW] = k
        r.qkv[at, 2 * HW :] = v
        r.qT[:, at] = q.T
        r.kT[:, at] = k.T
        r.vT[:, at] = v.T

    project(m)
    count_next()
    for j in range(C):
        ag[j][1].wait()
    project(mc)
    count_next()
    fw = {}
    for j in range(C):
        ag[j][0].wait()
        fw[j] = ag_forward(0, j, r.g1)
    project(mx)
    for j in range(C):
        fw[j].wait()
    project(md)

    pair_row = lax.broadcasted_iota(jnp.int32, (2 * HD, BQ), 0) // HD
    pair_lane = lax.broadcasted_iota(jnp.int32, (BQ, 2 * HD), 1) // HD
    scale2 = log2_e / math.sqrt(HD)
    K_AT, V_AT, Q_AT, DIST = 0, HW, 2 * HW, 3 * HW

    def make_dist(i):
        def one(b, carry):
            key = lax.broadcasted_iota(jnp.int32, (BQ, BQ), 0) + b * BQ
            query = lax.broadcasted_iota(jnp.int32, (BQ, BQ), 1) + i * BQ
            apart = query - key
            key_seg = r.segr[:, pl.ds(pl.multiple_of(b * BQ, BQ), BQ)]
            key_seg = jnp.broadcast_to(key_seg, (BQ, BQ)).T
            same = key_seg == r.segr[:, i * BQ : (i + 1) * BQ]
            r.big[b, :, DIST : DIST + BQ] = jnp.where((apart >= 0) & same, apart.astype(F32), jnp.inf)
            return carry

        lax.fori_loop(0, i + 1, one, 0)

    def head_slope(h):
        head = jnp.zeros((1, BQ), jnp.int32) + (m * LOCAL_HEADS + h + 1)
        return jnp.exp2(head.astype(F32) * (-8.0 / HEADS)) * log2_e

    def pair_lanes(h, start):
        return pl.ds(pl.multiple_of(start + (h // 2) * 2 * HD, 2 * HD), 2 * HD)

    def head_scores(i, ke, h):
        mask = (pair_row == lax.rem(h, 2)).astype(F32).astype(BF16)
        q_cols = r.qT[pair_lanes(h, 0), i * BQ : (i + 1) * BQ] * mask
        raw = mm(r.qkv[0:ke, pair_lanes(h, HW)], q_cols, NN)
        return raw * scale2 - head_slope(h) * r.big[0 : i + 1, :, DIST : DIST + BQ].reshape(ke, BQ)

    n_blocks = T // BQ
    for i in range(n_blocks):
        ke = (i + 1) * BQ
        block = slice(i * BQ, (i + 1) * BQ)
        make_dist(i)

        def head_body(h, carry):
            s = head_scores(i, ke, h)
            top = jnp.max(s, 0, keepdims=True)
            e = jnp.exp2(s - top)
            total = jnp.sum(e, 0, keepdims=True)
            p = (e * (1.0 / total)).astype(BF16)
            r.lse[h, :, block] = top + jnp.log2(total)
            at = pl.ds(pl.multiple_of(h * HD, HD), HD)
            r.mixT[at, :] = mm(r.vT[at, 0:ke], p, NN).astype(BF16)
            return carry

        lax.fori_loop(0, LOCAL_HEADS, head_body, 0)
        r.mix[block, :] = r.mixT[...].T
        if i < len(bits) - 2:
            count_next()
    for _ in range(2 + n_blocks, len(bits)):
        count_next()

    def rows4(ref, j):
        v = ref[:, pl.ds(j * rc, rc), :]
        return v.reshape(v.shape[0] * rc, v.shape[2])

    def pair_rows(ref, j):
        def of(first):
            v = ref[pl.ds(first, 2), pl.ds(j * rc, rc), :]
            return v.reshape(2 * rc, v.shape[2])

        return of

    def pair_flat(ref, j):
        def of(first):
            a = ref[pl.ds(pl.multiple_of(first * R + j * rc, rc), rc), :]
            b = ref[pl.ds(pl.multiple_of(first * R + R + j * rc, rc), rc), :]
            return jnp.concatenate([a, b], 0)

        return of

    def ag_finish(site, j, ref):
        ag[j][0].wait()
        cf = ag_forward(site, j, ref)
        ag[j][1].wait()
        cf.wait()

    weights[1].wait()
    rs = {}
    for j in range(C):
        rs[j] = rs_start(0, j, pair_flat(r.mix, j), lambda lanes: (r.wout[:, lanes], NN))
    for j in range(C):
        rows = slice(j * rc, (j + 1) * rc)
        hid = r.x[rows, :].astype(F32) + rs_finish(j, rs[j]) + r.vec[2:3, :]
        r.hidden[rows, :] = hid
        normed, inverse = norm_rows(hid)
        r.n2[rows, :] = normed
        r.inv2[rows, :] = inverse
        ag[j] = ag_start(1, j, r.g2, (normed * r.vec[3:4, :] + r.vec[4:5, :]).astype(BF16))

    weights[2].wait()
    weights[3].wait()
    for j in range(C):
        ag_finish(1, j, r.g2)
        rows = rows4(r.g2, j)

        def up_body(n, carry):
            lanes = pl.ds(pl.multiple_of(n * TILE, TILE), TILE)
            u = mm(rows, r.wup[:, lanes], NN) + r.vec[pl.ds(8 + m, 1), lanes]
            a, b = gelu_both(u)
            r.act[:, pl.ds(j * rc, rc), lanes] = a.astype(BF16).reshape(mp_size, rc, TILE)
            r.big[:, pl.ds(j * rc, rc), lanes] = b.reshape(mp_size, rc, TILE)
            return carry

        lax.fori_loop(0, FU // TILE, up_body, 0)
        rs[j] = rs_start(1, j, pair_rows(r.act, j), lambda lanes: (r.wdown[:, lanes], NN))

    loss_scale = token_total / r.cnt[len(bits), 0:1, 0:1]
    for j in range(C):
        rows = slice(j * rc, (j + 1) * rc)
        out = r.hidden[rows, :] + rs_finish(j, rs[j]) + r.vec[5:6, :]
        r.bo[rows, :] = out.astype(BF16)
        grad = r.valid[rows, :] * (out - r.t[rows, :].astype(F32)) * loss_scale
        r.ig[rows, :] = grad
        ag[j] = ag_start(2, j, r.g3, grad.astype(BF16))
        r.vg[5:6, :] += jnp.sum(grad, 0, keepdims=True)

    for j in range(C):
        ag_finish(2, j, r.g3)
        if fast and j == C - 1:
            y_start("d")
        rows = rows4(r.g3, j)

        def act_body(n, carry):
            lanes = pl.ds(pl.multiple_of(n * TILE, TILE), TILE)
            ga = mm(rows, r.wdown[lanes, :], NT)
            gu = ga * r.big[:, pl.ds(j * rc, rc), lanes].reshape(mp_size * rc, TILE)
            r.gup[:, pl.ds(j * rc, rc), lanes] = gu.astype(BF16).reshape(mp_size, rc, TILE)
            return carry

        lax.fori_loop(0, FU // TILE, act_body, 0)
        rs[j] = rs_start(2, j, pair_rows(r.gup, j), lambda lanes: (r.wup[lanes, :], NT))

    def whole_grad(left, right, width, dst):
        def body(n, carry):
            lanes = pl.ds(pl.multiple_of(n * TILE, TILE), TILE)
            r.stage[:, 0:width] = mm(right_tile(left, lanes), right[...].reshape(T, width), TN)
            put_out(r.stage.at[:, 0:width], dst.at[lanes, :])
            return carry

        lax.fori_loop(0, dst.shape[0] // TILE, body, 0)

    if not fast:
        whole_grad(r.act, r.g3, D, r.d_grad)

    for j in range(C):
        rows = slice(j * rc, (j + 1) * rc)
        gs = rs_finish(j, rs[j])
        gh = r.ig[rows, :] + norm_backward(gs, r.n2[rows, :], r.inv2[rows, :], r.vec[3:4, :])
        r.hidden[rows, :] = gh
        ag[j] = ag_start(3, j, r.g4, gh.astype(BF16))
        r.vg[2:3, :] += jnp.sum(gh, 0, keepdims=True)
        r.vg[3:4, :] += jnp.sum(gs * r.n2[rows, :], 0, keepdims=True)
        r.vg[4:5, :] += jnp.sum(gs, 0, keepdims=True)

    if fast:
        y_start("u")
    else:
        whole_grad(r.g2, r.gup, FU, r.u_grad)
    r.vg[pl.ds(8 + m, 1), :] = jnp.sum(r.gup[...].reshape(T, FU).astype(F32), 0, keepdims=True)

    for j in range(C):
        ag_finish(3, j, r.g4)

    def gm_body(o, carry):
        at = pl.ds(pl.multiple_of(o * R, R), R)
        gmx = mm(r.g4[o], r.wout[...], NT).astype(BF16)
        r.gm[at, :] = gmx
        r.vT[:, at] = gmx.T
        return carry

    lax.fori_loop(0, mp_size, gm_body, 0)
    if fast:
        y_start("o")

    r.big[:, :, K_AT : K_AT + HW] = jnp.zeros((mp_size, R, HW), F32)
    r.big[:, :, V_AT : V_AT + HW] = jnp.zeros((mp_size, R, HW), F32)
    for i in range(n_blocks):
        ke = (i + 1) * BQ
        block = slice(i * BQ, (i + 1) * BQ)
        make_dist(i)

        def back_body(h, carry):
            lanes = pair_lanes(h, 0)
            row_mask = (pair_row == lax.rem(h, 2)).astype(F32).astype(BF16)
            lane_mask = (pair_lane == lax.rem(h, 2)).astype(F32).astype(BF16)
            p = jnp.exp2(head_scores(i, ke, h) - r.lse[h, :, block])
            gp = mm(r.qkv[0:ke, pair_lanes(h, 2 * HW)], r.vT[lanes, block] * row_mask, NN)
            inner = jnp.sum(p * gp, 0, keepdims=True)
            raw = (p * (gp - inner)).astype(BF16)
            low = p.astype(BF16)
            r.big[0 : i + 1, :, pair_lanes(h, V_AT)] += mm(
                low, r.gm[block, lanes] * lane_mask, NN
            ).reshape(i + 1, BQ, 2 * HD)
            r.big[0 : i + 1, :, pair_lanes(h, K_AT)] += mm(
                raw, r.qkv[block, lanes] * lane_mask, NN
            ).reshape(i + 1, BQ, 2 * HD)
            at = pl.ds(pl.multiple_of(h * HD, HD), HD)
            r.big[i, at, Q_AT : Q_AT + BQ] = mm(r.kT[at, 0:ke], raw, NN) * (1.0 / math.sqrt(HD))
            return carry

        lax.fori_loop(0, LOCAL_HEADS, back_body, 0)
        r.st[block, 0:HW] = r.big[i, 0:HW, Q_AT : Q_AT + BQ].T.astype(BF16)
        if fast and i >= 1:
            chain_step("d", i - 1)
    r.st[:, HW : 2 * HW] = (
        r.big[:, :, K_AT : K_AT + HW].reshape(T, HW) * (1.0 / math.sqrt(HD))
    ).astype(BF16)
    r.st[:, 2 * HW :] = r.big[:, :, V_AT : V_AT + HW].reshape(T, HW).astype(BF16)
    r.vg[6:7, head_lanes] = jnp.sum(r.st[:, 0:HW].astype(F32), 0, keepdims=True)
    r.vg[7:8, head_lanes] = jnp.sum(r.st[:, 2 * HW :].astype(F32), 0, keepdims=True)

    if fast:
        fetch_state("u")
        fetch_state("q")

    for j in range(C):
        rs[j] = rs_start(3, j, pair_flat(r.st, j), lambda lanes: (r.wqkv[lanes, :], NT))

    if fast:
        y_start("q")
        chain_step("u", 0)
        finish_share("d")
    else:
        whole_grad(r.mix, r.g4, D, r.o_grad)
        whole_grad(r.g1, r.st, 3 * HW, r.q_grad)

    for j in range(C):
        rows = slice(j * rc, (j + 1) * rc)
        gf = rs_finish(j, rs[j])
        normed, inverse = norm_rows(r.x[rows, :].astype(F32))
        r.ig[rows, :] = r.hidden[rows, :] + norm_backward(gf, normed, inverse, r.vec[0:1, :])
        r.vg[0:1, :] += jnp.sum(gf * normed, 0, keepdims=True)
        r.vg[1:2, :] += jnp.sum(gf, 0, keepdims=True)

    vector_send, vector_next = doubling(r.vs, r.vs_r, r.vs_ss, r.vs_rs)
    r.vs[0] = r.vg[...]
    vector_send(0)
    if fast:
        chain_step("u", 1)
        chain_step("o", 0)
        vector_next()
        gather_step("d", 1)
        chain_step("u", 2)
        chain_step("o", 1)
        chain_step("q", 0)
        vector_next()
        finish_share("u")
        gather_step("d", 2)
        chain_step("o", 2)
        chain_step("q", 1)
        vector_next()
        finish_share("o")
        gather_step("d", 3)
        gather_step("u", 1)
        chain_step("q", 2)
        gather_step("o", 1)
        vector_next()
        finish_share("q")
        gather_step("u", 2)
        gather_step("o", 2)
        gather_step("q", 1)
        gather_step("u", 3)
        gather_step("o", 3)
        gather_step("q", 2)
        vector_next()
        gather_step("q", 3)
        for name in ("d", "u", "o", "q"):
            gather_end(name)
        for cp in local_out:
            cp.wait()
    else:
        for _ in bits:
            vector_next()
    r.vsum[...] = r.vs[len(bits)]


SHARE = 128


def block_call(sizes, x, teacher, segments, valid, vectors, copies, states):
    dp_size, mp_size = sizes
    R, D = x.shape
    T = mp_size * R
    wqkv, wout, wup, wdown = copies
    HW = wout.shape[0]
    FU = wup.shape[1]
    C = CHUNKS
    rc = R // C
    n_bits = (dp_size * mp_size).bit_length() - 1
    NZ = dp_size // 2
    fast = D == dp_size * SHARE
    dma = pltpu.SemaphoreType.DMA
    V = pltpu.VMEM
    S = jax.ShapeDtypeStruct
    vmem = pl.BlockSpec(memory_space=pltpu.VMEM)
    anywhere = pl.BlockSpec(memory_space=pl.ANY)

    ins = {
        "x": (x, vmem),
        "t": (teacher, vmem),
        "segr": (segments.reshape(1, T), vmem),
        "valid": (valid.reshape(R, 1), vmem),
        "vec": (vectors, vmem),
        "wqkv_hbm": (wqkv, anywhere),
        "wout_hbm": (wout, anywhere),
        "wup_hbm": (wup, anywhere),
        "wdown_hbm": (wdown, anywhere),
    }
    outs = {
        "bo": (S((R, D), BF16), vmem),
        "ig": (S((R, D), F32), vmem),
        "vsum": (S((16, D), F32), vmem),
    }
    if fast:
        shard = {"q": (SHARE, 3 * HW), "o": (HW, SHARE), "u": (SHARE, FU), "d": (FU, SHARE)}
        whole = {"q": (D, 3 * HW), "o": (HW, D), "u": (D, FU), "d": (FU, D)}
        for name, state in zip("qoud", states):
            ins["s%s_hbm" % name] = (state, anywhere)
        for name in "qoud":
            outs[name + "_grad"] = (S(shard[name], F32), anywhere)
        for name in "qoud":
            outs[name + "_new"] = (S((3,) + shard[name], F32), anywhere)
        for name in "qoud":
            outs[name + "_full"] = (S(whole[name], BF16), anywhere)
    else:
        outs["q_grad"] = (S((D, 3 * HW), F32), anywhere)
        outs["o_grad"] = (S((HW, D), F32), anywhere)
        outs["u_grad"] = (S((D, FU), F32), anywhere)
        outs["d_grad"] = (S((FU, D), F32), anywhere)
    scratch = {
        "wqkv": V((D, 3 * HW), BF16),
        "wout": V((HW, D), BF16),
        "wup": V((D, FU), BF16),
        "wdown": V((FU, D), BF16),
        "w_sem": dma((4,)),
        "g1": V((mp_size, R, D), BF16),
        "g2": V((mp_size, R, D), BF16),
        "g3": V((mp_size, R, D), BF16),
        "g4": V((mp_size, R, D), BF16),
        "qkv": V((T, 3 * HW), BF16),
        "qT": V((HW, T), BF16),
        "kT": V((HW, T), BF16),
        "vT": V((HW, T), BF16),
        "mixT": V((HW, BQ), BF16),
        "mix": V((T, HW), BF16),
        "lse": V((HW // HD, 1, T), F32),
        "hidden": V((R, D), F32),
        "n2": V((R, D), F32),
        "inv2": V((R, 1), F32),
        "act": V((mp_size, R, FU), BF16),
        "big": V((mp_size, R, FU), F32),
        "gup": V((mp_size, R, FU), BF16),
        "gm": V((T, HW), BF16),
        "st": V((T, 3 * HW), BF16),
        "pass_on": V((C, rc, D), F32),
        "keep": V((C, rc, D), F32),
        "rs_cs": V((C, 2, rc, D), BF16),
        "rs_cr": V((C, 2, rc, D), BF16),
        "rs_xs": V((C, rc, D), BF16),
        "rs_xr": V((C, rc, D), BF16),
        "cnt": V((n_bits + 1, 8, 128), F32),
        "cnt_r": V((n_bits, 8, 128), F32),
        "vg": V((16, D), F32),
        "vs": V((n_bits + 1, 16, D), F32),
        "vs_r": V((n_bits, 16, D), F32),
        "ag_ss": dma((4, C, 3)),
        "ag_rs": dma((4, C, 3)),
        "rs_ss": dma((4, C, 3)),
        "rs_rs": dma((4, C, 3)),
        "cnt_ss": dma((n_bits,)),
        "cnt_rs": dma((n_bits,)),
        "vs_ss": dma((n_bits,)),
        "vs_rs": dma((n_bits,)),
    }
    if fast:
        wide = {"q": 3 * HW, "o": HW, "u": FU, "d": FU}
        for name in "qoud":
            w = wide[name]
            scratch["ys" + name] = V((NZ, SHARE, w), BF16)
            scratch["yr" + name] = V((NZ, SHARE, w), BF16)
            scratch["zs" + name] = V((2, SHARE, w), BF16)
            scratch["zr" + name] = V((2, NZ - 1, SHARE, w), BF16)
            if name in "od":
                scratch["s" + name] = V((3,) + shard[name], F32)
            scratch["gr" + name] = V(shard[name], F32)
            scratch["nc" + name] = V(shard[name], BF16)
        scratch["acc"] = V((SHARE, FU), F32)
        scratch["s_sem"] = dma((4,))
        scratch["o_sem"] = dma((4, 3))
        scratch["y_ss"] = dma((4, NZ))
        scratch["y_rs"] = dma((4, NZ))
        scratch["z_ss"] = dma((4, 2, NZ - 1))
        scratch["z_rs"] = dma((4, 2, NZ - 1))
        scratch["az_ss"] = dma((4, 2, NZ - 1))
        scratch["az_rs"] = dma((4, 2, NZ - 1))
        scratch["ay_ss"] = dma((4, NZ))
        scratch["ay_rs"] = dma((4, NZ))
    else:
        scratch["stage"] = V((TILE, D), F32)
        scratch["stage_sem"] = dma
    names = list(ins) + list(outs) + list(scratch)
    results = pl.pallas_call(
        functools.partial(block_kernel, sizes, fast, names),
        out_shape=[v[0] for v in outs.values()],
        in_specs=[v[1] for v in ins.values()],
        out_specs=[v[1] for v in outs.values()],
        scratch_shapes=list(scratch.values()),
        compiler_params=pltpu.CompilerParams(
            collective_id=0, has_side_effects=True, vmem_limit_bytes=62 << 20
        ),
        name="block",
    )(*[v[0] for v in ins.values()])
    return dict(zip(outs, results)), fast


def adam_update(gradient, stored, decay_factor, token_total):
    new = adam_step(gradient, stored[0], stored[1], stored[2], decay_factor, token_total)
    return (jnp.stack(new), new[0].astype(jnp.bfloat16))


def shards(
    inputs,
    teacher,
    segments,
    valid_mask,
    qkv_copy,
    out_copy,
    up_copy,
    down_copy,
    vector_copy,
    qkv_state,
    out_state,
    up_state,
    down_state,
    vector_state,
):
    sizes = (lax.axis_size("dp"), lax.axis_size("mp"))
    token_total = inputs.shape[0] * sizes[0] * sizes[1]
    width = inputs.shape[1]
    head_width = qkv_copy.shape[2]
    outs, fast = block_call(
        sizes,
        inputs,
        teacher,
        segments,
        valid_mask.astype(F32),
        vector_copy.astype(F32),
        (qkv_copy.reshape(width, 3 * head_width), out_copy, up_copy, down_copy),
        (
            qkv_state.reshape(qkv_state.shape[:2] + (3 * head_width,)),
            out_state,
            up_state,
            down_state,
        ),
    )
    vector_grad = outs["vsum"][: vector_copy.shape[0]]
    vector_new, vector_low = adam_update(vector_grad, vector_state, 0.0, token_total)
    if fast:
        qkv_grad = outs["q_grad"].reshape(qkv_state.shape[1:])
        out_grad, up_grad, down_grad = (outs[n + "_grad"] for n in "oud")
        qkv_new = outs["q_new"].reshape(qkv_state.shape)
        out_new, up_new, down_new = (outs[n + "_new"] for n in "oud")
        qkv_full = outs["q_full"].reshape(qkv_copy.shape)
        out_full, up_full, down_full = (outs[n + "_full"] for n in "oud")
    else:
        qkv_local = outs["q_grad"].reshape(width, 3, head_width)
        qkv_grad, out_grad, up_grad, down_grad = (
            lax.psum_scatter(qkv_local, "dp", scatter_dimension=0, tiled=True),
            lax.psum_scatter(outs["o_grad"], "dp", scatter_dimension=1, tiled=True),
            lax.psum_scatter(outs["u_grad"], "dp", scatter_dimension=0, tiled=True),
            lax.psum_scatter(outs["d_grad"], "dp", scatter_dimension=1, tiled=True),
        )
        qkv_new, qkv_low = adam_update(qkv_grad, qkv_state, decay_rate, token_total)
        out_new, out_low = adam_update(out_grad, out_state, decay_rate, token_total)
        up_new, up_low = adam_update(up_grad, up_state, decay_rate, token_total)
        down_new, down_low = adam_update(down_grad, down_state, decay_rate, token_total)
        qkv_full, out_full, up_full, down_full = (
            lax.all_gather(qkv_low, "dp", axis=0, tiled=True),
            lax.all_gather(out_low, "dp", axis=1, tiled=True),
            lax.all_gather(up_low, "dp", axis=0, tiled=True),
            lax.all_gather(down_low, "dp", axis=1, tiled=True),
        )
    return (
        outs["bo"],
        outs["ig"],
        qkv_grad,
        out_grad,
        up_grad,
        down_grad,
        vector_grad,
        qkv_new,
        out_new,
        up_new,
        down_new,
        vector_new,
        qkv_full,
        out_full,
        up_full,
        down_full,
        vector_low,
    )


def solution(mesh):
    in_specs = (
        P(("dp", "mp"), None),
        P(("dp", "mp"), None),
        P("dp", None),
        P(("dp", "mp")),
        P(None, None, "mp"),
        P("mp", None),
        P(None, "mp"),
        P("mp", None),
        P(),
        P(None, "dp", None, "mp"),
        P(None, "mp", "dp"),
        P(None, "dp", "mp"),
        P(None, "mp", "dp"),
        P(),
    )
    out_specs = (
        P(("dp", "mp"), None),
        P(("dp", "mp"), None),
        P("dp", None, "mp"),
        P("mp", "dp"),
        P("dp", "mp"),
        P("mp", "dp"),
        P(),
        P(None, "dp", None, "mp"),
        P(None, "mp", "dp"),
        P(None, "dp", "mp"),
        P(None, "mp", "dp"),
        P(),
        P(None, None, "mp"),
        P("mp", None),
        P(None, "mp"),
        P("mp", None),
        P(),
    )
    return jax.shard_map(shards, mesh=mesh, in_specs=in_specs, out_specs=out_specs, check_vma=False)
```

time: 658 us -> 275 us (0.42)
  waiting for transfers between devices: 385 us -> 0 us
  Pallas kernels: 149 us -> 244 us
  blocking collectives: 70.3 us -> 0 us
  between operations: 14.3 us -> 0.78 us
  other arithmetic: 16.3 us -> 4.4 us
    reduce_scatter x4 -> x0, waiting for transfers between devices: 273 us -> none  [the longest x1 90.6 us: shards(): lax.psum_scatter(down_local, 'dp', scatter_dimension=1, tiled=True)]
    all_gather x3 -> x0, waiting for transfers between devices: 110 us -> none  [the longest x1 52.4 us: shards(): lax.all_gather(down_low, 'dp', axis=1, tiled=True)]
    pallas_call x1, Pallas kernels: 149 us -> 244 us  [block_call(): pl.pallas_call(functools.partial(block_kernel, sizes, fast, names), out_s...]
    psum x1 -> x0, blocking collectives: 40.8 us -> none  [shards(): vector_grad = lax.psum(vector_local[:vector_copy.shape[0]], ('dp', 'mp'))]
    all_gather x1 -> x0, blocking collectives: 29.5 us -> none  [shards(): lax.all_gather(out_low, 'dp', axis=1, tiled=True)]
    convert_element_type x5 -> x1, other arithmetic: 9.13 us -> 1.61 us  [adam_update(): return (jnp.stack(new), new[0].astype(jnp.bfloat16))]
    unnamed x40 -> x48, local copies, waits for them, and re-layouts: 14.6 us -> 19.5 us
  transfers between devices with their start and end apart: 7 -> 0, of which waited for: 7 -> 0; matrix products, arithmetic and copies ran while one was open for 3% -> 0% of each run, Pallas kernels for 0% -> 0%
where the time goes in v2:
time: 275 us; the launch traced here: 274 us
  Pallas kernels  244 us (89%)
  local copies, waits for them, and re-layouts  25.5 us (9%)
  other arithmetic  4.4 us (2%)
    pallas_call x1, Pallas kernels, block_call(): pl.pallas_call(functools.partial(block_kernel, sizes, fast, names), out_s...  244 us
    unnamed x48, local copies, waits for them, and re-layouts  19.5 us

profile of v2, /device:TPU:0, one launch (start us, length us, event | category | flops | bytes accessed | tf_op | source)
XLA Modules:
  0.0 274.5 jit_solution(14207009214538998017)
XLA Ops:
  0.7 0.7 convert_element_type.9
  1.3 1.4 convert_element_type.10.refs_4_
  2.7 0.8 copy.38.refs_3_
  3.5 1.6 copy.37
  5.2 0.0 copy-start.2
  5.2 1.4 copy.40.refs_9_
  6.6 0.2 copy-done.2
  6.8 0.9 copy.36
  7.6 1.6 copy.39.refs_5_
  9.2 243.8 %block.1 = (bf16[256,1024]{1,0:T(8,128)(2,1)}, f32[256,1024]{1,0:T(8,128)}, f32[16,1024]{1,0:T(8,128)}, f32[128,768]{1,0:T(8,128)}, f32[256,128]{1,0:T(8,128)}, ...) custom-call(bf16[256,1024]{1,0:T(8,128)(2,1)} %refs_0_.1, ...), custom_call_target="tpu_custom_call" | custom-call | tf_op jit(solution)/shard_map/block/pallas_call | solution.py:920
  253.0 0.0 copy-start.6
  253.0 0.0 copy-done.8
  253.0 1.6 fusion.4
  254.6 0.7 pad_maximum_fusion
  255.3 1.1 copy.41
  256.5 0.9 copy.44
  257.4 0.0 copy-done.6
  257.4 0.4 copy.42
  257.8 0.0 copy-done.14
  257.8 0.0 copy-start.5
  257.8 1.4 copy.45
  259.2 0.2 copy-done.5
  259.4 0.7 copy.43
  260.1 0.0 copy-start.12
  260.1 0.0 copy-start.7
  260.2 1.6 copy.46
  261.7 0.0 copy-done.12
  261.7 0.8 copy.58
  262.5 0.0 copy-done.7
  262.5 1.0 copy.59
  263.5 0.0 copy-done.15
  263.5 0.7 copy.60
  264.2 0.0 copy-done.11
  264.2 0.8 copy.61
  265.0 0.0 copy-done.10
  265.0 0.8 copy.62
  265.8 0.0 copy-done.13
  265.8 0.7 copy.63
  266.5 0.0 copy-done.4
  266.5 1.1 copy.64
  267.7 0.8 copy-done.3
  268.5 1.1 copy.65
  269.6 0.2 copy-done.9
  269.9 0.8 copy.66
  270.7 0.2 copy-done.1
  270.8 1.3 copy.67
  272.1 1.0 copy-done
  273.2 1.3 copy.68
  (12 shorter events, 0.0 us)
Async XLA Ops:
  5.2 1.6 copy-start.2
  9.2 243.8 %copy-start.8 = (f32[3,12,1024]{2,1,0:T(8,128)S(1)}, f32[3,12,1024]{2,1,0:T(8,128)}, u32[]{:S(2)}) copy-start(f32[3,12,1024]{2,1,0:T(8,128)} %param.27) | copy-start | bytes 442372
  253.0 4.4 %copy-start.6 = (f32[3,128,768]{2,1,0:T(8,128)S(1)}, f32[3,128,768]{2,1,0:T(8,128)}, u32[]{:S(2)}) copy-start(f32[3,128,768]{2,1,0:T(8,128)} %get-tuple-element.39) | copy-start | bytes 3538948
  254.6 3.2 %copy-start.14 = (f32[12,1024]{1,0:T(8,128)}, f32[12,1024]{1,0:T(8,128)S(1)}, u32[]{:S(2)}) copy-start(f32[12,1024]{1,0:T(8,128)S(1)} %get-tuple-element.109) | copy-start | bytes 147460
  257.8 1.6 copy-start.5
  260.1 1.6 copy-start.12
  260.1 2.4 copy-start.7
  261.7 1.8 copy-start.15
  261.7 2.4 copy-start.11
  262.5 2.4 copy-start.10
  263.5 2.3 copy-start.13
  263.5 3.0 %copy-start.4 = (f32[3,128,1024]{2,1,0:T(8,128)S(1)}, f32[3,128,1024]{2,1,0:T(8,128)}, u32[]{:S(2)}) copy-start(f32[3,128,1024]{2,1,0:T(8,128)} %get-tuple-element.112) | copy-start | bytes 4718596
  266.5 2.0 copy-start.3
  268.5 1.4 copy-start.9
  268.5 2.3 copy-start.1
  270.8 2.3 copy-start

commit v3 on v2

--- a/solution.py
+++ b/solution.py
@@ -89,10 +89,13 @@
     HW = r.wout.shape[0]
     FU = r.wup.shape[1]
     LOCAL_HEADS = HW // HD
+    PAIR = 2 * HD
+    PAIRS = HW // PAIR
     token_total = float(dp_size * T)
 
-    bits = [("mp", b) for b in range(mp_size.bit_length() - 1)]
-    bits += [("dp", b) for b in range(dp_size.bit_length() - 1)]
+    dp_bits = [("dp", b) for b in range(dp_size.bit_length() - 1)]
+    mp_bits = [("mp", b) for b in range(mp_size.bit_length() - 1)]
+    bits = dp_bits + mp_bits
 
     def flip(v, b):
         w = 1 << b
@@ -121,31 +124,69 @@
         cp.start()
         return cp
 
+    def qkv_lanes(pair, kind):
+        return slice((3 * pair + kind) * PAIR, (3 * pair + kind + 1) * PAIR)
+
+    qkv_weights = [
+        local_copy(
+            r.wqkv_hbm.at[kind, :, pair * PAIR : (pair + 1) * PAIR],
+            r.wqkv.at[:, qkv_lanes(pair, kind)],
+            r.wq_sem.at[pair, kind],
+        )
+        for pair in range(PAIRS)
+        for kind in range(3)
+    ]
     weights = [
         local_copy(src, dst, r.w_sem.at[i])
         for i, (src, dst) in enumerate(
-            [(r.wqkv_hbm, r.wqkv), (r.wout_hbm, r.wout), (r.wup_hbm, r.wup), (r.wdown_hbm, r.wdown)]
+            [(r.wout_hbm, r.wout), (r.wup_hbm, r.wup), (r.wdown_hbm, r.wdown)]
         )
     ]
     if fast:
-        parts = {
-            "d": (0, r.g3, r.act, FU, True),
-            "u": (1, r.g2, r.gup, FU, False),
-            "o": (2, r.g4, r.mix, HW, True),
-            "q": (3, r.g1, r.st, 3 * HW, False),
-        }
-        states = {
-            "d": r.sd,
-            "u": r.big.at[0:3, 0:SHARE, :],
-            "o": r.so,
-            "q": r.big.at[0:3, SHARE : 2 * SHARE, 0 : 3 * HW],
-        }
+        parts = {}
+        for name, width in pieces(HW, FU):
+            left, right = {
+                "d": (r.g3, r.act),
+                "u": (r.g2, r.gup),
+                "o": (r.g4, r.mix),
+                "q": (r.g1, r.st),
+            }[name[0]]
+            parts[name] = (len(parts), left, right, width)
         state_in = {}
 
-        def fetch_state(name):
-            state_in[name] = local_copy(
-                getattr(r, "s%s_hbm" % name), states[name], r.s_sem.at[parts[name][0]]
-            )
+        def span(name):
+            width = PAIR if name[0] == "q" else parts[name][3]
+            return slice(int(name[1]) * width, (int(name[1]) + 1) * width)
+
+        def piece(ref, name):
+            at = span(name)
+            if name[0] == "q":
+                return ref.at[:, :, at]
+            return ref.at[:, at] if name[0] == "u" else ref.at[at, :]
+
+        def state_copies(name, out):
+            far = getattr(r, name[0] + "_new") if out else getattr(r, "s%s_hbm" % name[0])
+            at = span(name)
+            if name[0] == "q":
+                return [
+                    (
+                        far.at[:, kind, :, at],
+                        r.big.at[0:3, SHARE : 2 * SHARE, kind * HW + at.start : kind * HW + at.stop],
+                    )
+                    for kind in range(3)
+                ]
+            if name[0] == "u":
+                return [(far.at[:, :, at], r.big.at[0:3, 0:SHARE, at])]
+            return [(far.at[:, at, :], getattr(r, "s" + name[0]).at[:, at, :])]
+
+        def fetch_state(matrix):
+            for name in parts:
+                if name[0] == matrix:
+                    p = parts[name][0]
+                    state_in[name] = [
+                        local_copy(far, near, r.s_sem.at[p, k])
+                        for k, (far, near) in enumerate(state_copies(name, False))
+                    ]
 
         fetch_state("d")
         fetch_state("o")
@@ -165,14 +206,14 @@
         greetings = greetings + (z > 0).astype(jnp.int32) + (z < NZ - 1).astype(jnp.int32)
     pl.semaphore_wait(barrier, greetings)
 
-    def doubling(values, received, send_sems, recv_sems):
+    def doubling(order, values, received, send_sems, recv_sems):
         copies = []
 
         def send(step):
             cp = pltpu.make_async_remote_copy(
                 src_ref=values.at[step], dst_ref=received.at[step],
                 send_sem=send_sems.at[step], recv_sem=recv_sems.at[step],
-                device_id=bit_partner(bits[step]), device_id_type=MESH,
+                device_id=bit_partner(order[step]), device_id_type=MESH,
             )
             cp.start()
             copies.append(cp)
@@ -181,14 +222,15 @@
             step = len(copies) - 1
             copies[step].wait()
             values[step + 1] = values[step] + received[step]
-            if step + 1 < len(bits):
+            if step + 1 < len(order):
                 send(step + 1)
 
         return send, following
 
-    count_send, count_next = doubling(r.cnt, r.cnt_r, r.cnt_ss, r.cnt_rs)
-    r.cnt[0] = jnp.zeros((8, 128), F32) + jnp.sum(r.valid[...])
+    count_send, count_next = doubling(bits, r.cnt, r.cnt_r, r.cnt_ss, r.cnt_rs)
+    r.cnt[0] = jnp.zeros((8, 128), F32) + jnp.sum(r.valid[...].astype(F32))
     count_send(0)
+    r.vec[...] = r.vec_low[...].astype(F32)
 
     def ag_copy(site, j, kind, ref, block, device):
         part = ref.at[block, pl.ds(j * rc, rc)]
@@ -254,8 +296,28 @@
 
     def right_tile(ref, lanes):
         if len(ref.shape) == 3:
-            return ref[:, :, lanes].reshape(T, TILE)
+            return ref[:, :, lanes].reshape(T, lanes.size)
         return ref[:, lanes]
+
+    def tiles(width):
+        return width if width < 2 * TILE else TILE
+
+    def part_tile(name, n, step):
+        _, _, right, width = parts[name]
+        lanes = pl.ds(pl.multiple_of(n * step, 128), step)
+        from_lanes = pl.ds(pl.multiple_of(int(name[1]) * width + n * step, 128), step)
+        return lanes, right_tile(right, from_lanes)
+
+    def part_product(name, lhs, put):
+        width = parts[name][3]
+        step = tiles(width)
+
+        def tile_body(n, carry):
+            lanes, rhs = part_tile(name, n, step)
+            put(lanes, mm(lhs, rhs, NN))
+            return carry
+
+        lax.fori_loop(0, width // step, tile_body, 0)
 
     def y_copy(name, i):
         p = parts[name][0]
@@ -265,7 +327,7 @@
         )
 
     def y_start(name):
-        _, left, right, width, _ = parts[name]
+        left = parts[name][1]
         out = getattr(r, "ys" + name)
 
         def pair_body(i, carry):
@@ -273,32 +335,33 @@
                 [share_rows(left, 4 * i + 1 - y), share_rows(left, 4 * i + 3 - y)], 0
             )
 
-            def tile_body(n, inner):
-                lanes = pl.ds(pl.multiple_of(n * TILE, TILE), TILE)
-                both = mm(lhs, right_tile(right, lanes), NN).astype(BF16)
-                out[2 * i, :, lanes] = both[:SHARE]
-                out[2 * i + 1, :, lanes] = both[SHARE:]
-                return inner
-
-            lax.fori_loop(0, width // TILE, tile_body, 0)
+            def put(lanes, both):
+                out[2 * i, :, lanes] = both[:SHARE].astype(BF16)
+                out[2 * i + 1, :, lanes] = both[SHARE:].astype(BF16)
+
+            part_product(name, lhs, put)
             y_copy(name, 2 * i).start()
             y_copy(name, 2 * i + 1).start()
             return carry
 
         lax.fori_loop(0, NZ // 2, pair_body, 0)
 
-    def share_sum(name, target, put):
-        _, left, right, width, _ = parts[name]
+    def share_sum(name, target):
         got = getattr(r, "yr" + name)
         y_copy(name, target).wait_recv()
-        lhs = share_rows(left, 2 * target + y)
-
-        def tile_body(n, carry):
-            lanes = pl.ds(pl.multiple_of(n * TILE, TILE), TILE)
-            put(lanes, mm(lhs, right_tile(right, lanes), NN) + got[target, :, lanes].astype(F32))
-            return carry
-
-        lax.fori_loop(0, width // TILE, tile_body, 0)
+
+        def put(lanes, value):
+            r.acc[0:SHARE, lanes] = value + got[target, :, lanes].astype(F32)
+
+        part_product(name, share_rows(parts[name][1], 2 * target + y), put)
+
+    def both_shares(name, target):
+        def put(lanes, value):
+            r.wide[:, lanes] = value
+
+        left = parts[name][1]
+        lanes = pl.ds(pl.multiple_of(2 * target * SHARE, 2 * SHARE), 2 * SHARE)
+        part_product(name, left[:, :, lanes].reshape(T, 2 * SHARE).T, put)
 
     def z_copy(name, direction, step, device):
         p = parts[name][0]
@@ -312,6 +375,8 @@
     def chain_step(name, step):
         out = getattr(r, "zs" + name)
         got = getattr(r, "zr" + name)
+        width = parts[name][3]
+        total = (r.wide if name in Z_FIRST else r.acc).at[:, 0:width]
 
         def one(direction, carry):
             place, following = line(direction)
@@ -320,11 +385,7 @@
             def _():
                 mirrored = NZ - 1 - step + place
                 target = mirrored + direction * (NZ - 1 - 2 * mirrored)
-
-                def put(lanes, value):
-                    r.acc[:, lanes] = value
-
-                share_sum(name, target, put)
+                (both_shares if name in Z_FIRST else share_sum)(name, target)
                 if step > 0:
 
                     @pl.when(place < step)
@@ -334,29 +395,52 @@
                     @pl.when(place > 0)
                     def _():
                         z_copy(name, direction, step - 1, following).wait_recv()
-                        r.acc[:, 0 : out.shape[2]] += got[direction, step - 1].astype(F32)
-
-                out[direction] = r.acc[:, 0 : out.shape[2]].astype(BF16)
+                        total[...] += got[direction, step - 1].astype(F32)
+
+                out[direction] = total[...].astype(BF16)
                 z_copy(name, direction, step, following).start()
 
             return carry
 
         lax.fori_loop(0, 2, one, 0)
 
-    gathered = {}
+    def chain_end(name):
+        got = getattr(r, "zr" + name)
+        width = parts[name][3]
+        total = (r.wide if name in Z_FIRST else r.acc).at[:, 0:width]
+        (both_shares if name in Z_FIRST else share_sum)(name, z)
+
+        def one(direction, carry):
+            place, _ = line(direction)
+
+            @pl.when(place > 0)
+            def _():
+                z_copy(name, direction, NZ - 2, (dp, m)).wait_recv()
+                total[...] += got[direction, NZ - 2].astype(F32)
+
+            return carry
+
+        lax.fori_loop(0, 2, one, 0)
+
+    def y_exchange(name):
+        chain_end(name)
+        width = parts[name][3]
+        theirs = pl.ds(pl.multiple_of((1 - y) * SHARE, SHARE), SHARE)
+        getattr(r, "ys" + name)[0] = r.wide[theirs, 0:width].astype(BF16)
+        y_copy(name, 0).start()
 
     def a_src(name, share):
-        ref = getattr(r, name + "_full")
+        ref = getattr(r, name[0] + "_full")
         at = pl.ds(pl.multiple_of(share * SHARE, SHARE), SHARE)
-        if parts[name][4]:
-            return ref.at[:, at]
-        return ref.at[at, :]
-
-    def az_copy(name, direction, step, share, src, device):
+        if name[0] == "q":
+            return ref.at[:, at, span(name)]
+        return ref.at[at, span(name)] if name[0] == "u" else ref.at[span(name), at]
+
+    def az_copy(name, side, direction, step, share, src, device):
         p = parts[name][0]
         return pltpu.make_async_remote_copy(
-            src_ref=src, dst_ref=a_src(name, share), send_sem=r.az_ss.at[p, direction, step],
-            recv_sem=r.az_rs.at[p, direction, step], device_id=device, device_id_type=MESH,
+            src_ref=src, dst_ref=a_src(name, share), send_sem=r.az_ss.at[p, side, direction, step],
+            recv_sem=r.az_rs.at[p, side, direction, step], device_id=device, device_id_type=MESH,
         )
 
     def ay_copy(name, place, src):
@@ -369,82 +453,113 @@
     local_out = []
 
     def finish_share(name):
-        p, _, _, width, turned = parts[name]
-        got = getattr(r, "zr" + name)
-        state = states[name]
-        grad_out = getattr(r, "gr" + name)
-        fresh = getattr(r, "nc" + name)
-
-        def put(lanes, value):
-            r.acc[:, lanes] = value
-
-        share_sum(name, z, put)
-
-        def one(direction, carry):
-            place, _ = line(direction)
-
-            @pl.when(place > 0)
-            def _():
-                z_copy(name, direction, NZ - 2, (dp, m)).wait_recv()
-                r.acc[:, 0:width] += got[direction, NZ - 2].astype(F32)
-
-            return carry
-
-        lax.fori_loop(0, 2, one, 0)
-        state_in[name].wait()
-
-        def adam_body(n, carry):
-            cols = pl.ds(pl.multiple_of(n * SHARE, SHARE), SHARE)
+        p, _, _, width = parts[name]
+        matrix = name[0]
+        at0 = span(name)
+        if name in Z_FIRST:
+            y_copy(name, 0).wait_recv()
+            ours = pl.ds(pl.multiple_of(y * SHARE, SHARE), SHARE)
+            r.acc[:, 0:width] = r.wide[ours, 0:width] + getattr(r, "yr" + name)[0].astype(F32)
+        else:
+            chain_end(name)
+        for cp in state_in[name]:
+            cp.wait()
+        grad_out = getattr(r, "gr" + matrix)
+        fresh = getattr(r, "nc" + matrix)
+
+        def adam_block(cols, at, state, state_at):
             grad = r.acc[:, cols]
-            if turned:
+            if matrix in "do":
                 grad = grad.T
-                at = (cols, slice(None))
-            else:
-                at = (slice(None), cols)
             grad_out[at] = grad
             w, a, b = adam_step(
-                grad, state[(0,) + at], state[(1,) + at], state[(2,) + at], decay_rate, token_total
+                grad,
+                state[(0,) + state_at],
+                state[(1,) + state_at],
+                state[(2,) + state_at],
+                decay_rate,
+                token_total,
             )
-            state[(0,) + at] = w
-            state[(1,) + at] = a
-            state[(2,) + at] = b
+            state[(0,) + state_at] = w
+            state[(1,) + state_at] = a
+            state[(2,) + state_at] = b
             fresh[at] = w.astype(BF16)
-            return carry
-
-        lax.fori_loop(0, width // SHARE, adam_body, 0)
+
+        if matrix == "q":
+            for kind in range(3):
+                adam_block(
+                    slice(kind * PAIR, (kind + 1) * PAIR),
+                    (kind, slice(None), at0),
+                    r.big,
+                    (slice(SHARE, 2 * SHARE), slice(kind * HW + at0.start, kind * HW + at0.stop)),
+                )
+        else:
+
+            def adam_body(n, carry):
+                cols = pl.ds(pl.multiple_of(n * SHARE, SHARE), SHARE)
+                there = pl.ds(pl.multiple_of(at0.start + n * SHARE, SHARE), SHARE)
+                if matrix == "u":
+                    adam_block(cols, (slice(None), there), r.big, (slice(0, SHARE), there))
+                else:
+                    at = (there, slice(None))
+                    adam_block(cols, at, getattr(r, "s" + matrix), at)
+                return carry
+
+            lax.fori_loop(0, width // SHARE, adam_body, 0)
+        fresh = piece(fresh, name)
+        if name in Y_FIRST:
+            ay_copy(name, z, fresh).start()
         for direction in range(2):
             place, following = line(direction)
 
             @pl.when(place < NZ - 1)
             def _():
-                az_copy(name, direction, 0, 2 * z + y, fresh, following).start()
-
-        ay_copy(name, z, fresh).start()
+                az_copy(name, 0, direction, 0, 2 * z + y, fresh, following).start()
+
+        if name not in Y_FIRST:
+            ay_copy(name, z, fresh).start()
         local_out.append(local_copy(fresh, a_src(name, 2 * z + y), r.o_sem.at[p, 0]))
-        local_out.append(local_copy(grad_out, getattr(r, name + "_grad"), r.o_sem.at[p, 1]))
-        local_out.append(local_copy(state, getattr(r, name + "_new"), r.o_sem.at[p, 2]))
-
-    def gather_step(name, step):
+        local_out.append(
+            local_copy(piece(grad_out, name), piece(getattr(r, matrix + "_grad"), name), r.o_sem.at[p, 1])
+        )
+        for k, (far, near) in enumerate(state_copies(name, True)):
+            local_out.append(local_copy(near, far, r.o_sem.at[p, 2 + k]))
+
+    def neighbour_share(name):
+        part = a_src(name, 2 * z + 1 - y)
+        ay_copy(name, z, part).wait_recv()
         for direction in range(2):
             place, following = line(direction)
 
-            @pl.when(place >= step)
+            @pl.when(place < NZ - 1)
             def _():
-                source = z - step + 2 * step * direction
-                part = a_src(name, 2 * source + y)
-                az_copy(name, direction, step - 1, 2 * source + y, part, following).wait_recv()
-                if step < NZ - 1:
-
-                    @pl.when(place < NZ - 1)
-                    def _():
-                        az_copy(name, direction, step, 2 * source + y, part, following).start()
-
-                ay_copy(name, source, part).start()
+                az_copy(name, 1, direction, 0, 2 * z + 1 - y, part, following).start()
+
+    def gather_step(name, step):
+        for side in range(2 if name in Y_FIRST else 1):
+            for direction in range(2):
+                place, following = line(direction)
+
+                @pl.when(place >= step)
+                def _():
+                    source = z - step + 2 * step * direction
+                    share = 2 * source + (1 - y if side else y)
+                    part = a_src(name, share)
+                    az_copy(name, side, direction, step - 1, share, part, following).wait_recv()
+                    if step < NZ - 1:
+
+                        @pl.when(place < NZ - 1)
+                        def _():
+                            az_copy(name, side, direction, step, share, part, following).start()
+
+                    if name not in Y_FIRST:
+                        ay_copy(name, source, part).start()
 
     def gather_end(name):
+        part = a_src(name, 2 * z + y)
+
         def one(direction, carry):
             place, following = line(direction)
-            part = a_src(name, 2 * z + y)
 
             @pl.when(place <= NZ - 2)
             def _():
@@ -454,17 +569,24 @@
 
                 @pl.when((place >= step) & (place < NZ - 1))
                 def _():
-                    az_copy(name, direction, step, 2 * z + y, part, following).wait_send()
+                    for side in range(2 if name in Y_FIRST else 1):
+                        az_copy(name, side, direction, step, 2 * z + y, part, following).wait_send()
 
             return carry
 
         lax.fori_loop(0, 2, one, 0)
+        if name in Z_FIRST:
+            y_copy(name, 0).wait_send()
+        if name in Y_FIRST:
+            ay_copy(name, z, part).wait_send()
 
         def y_body(i, carry):
-            y_copy(name, i).wait_send()
-            part = a_src(name, 2 * i + y)
-            ay_copy(name, i, part).wait_send()
-            ay_copy(name, i, part).wait_recv()
+            if name not in Z_FIRST:
+                y_copy(name, i).wait_send()
+            if name not in Y_FIRST:
+                there = a_src(name, 2 * i + y)
+                ay_copy(name, i, there).wait_send()
+                ay_copy(name, i, there).wait_recv()
             return carry
 
         lax.fori_loop(0, NZ, y_body, 0)
@@ -473,6 +595,28 @@
         cp = pltpu.make_async_copy(src, dst, r.stage_sem)
         cp.start()
         cp.wait()
+
+    late = {}
+
+    def turn(point):
+        if not fast:
+            return
+        for item in ORDER.get(point, "").split():
+            kind, rest = item[0], item[1:]
+            if kind == "v":
+                late["vector_next"]()
+            elif kind == "y":
+                y_start(rest)
+            elif kind == "f":
+                finish_share(rest)
+            elif kind == "e":
+                y_exchange(rest)
+            elif kind == "h":
+                neighbour_share(rest)
+            elif kind == "c":
+                chain_step(rest[1:], int(rest[0]))
+            elif kind == "g":
+                gather_step(rest[1:], int(rest[0]))
 
     r.vg[...] = jnp.zeros(r.vg.shape, F32)
     ag = {}
@@ -482,27 +626,32 @@
         ag[j] = ag_start(0, j, r.g1, (normed * r.vec[0:1, :] + r.vec[1:2, :]).astype(BF16))
 
     head_lanes = pl.ds(pl.multiple_of(m * HW, HW), HW)
-    weights[0].wait()
+    for w in qkv_weights:
+        w.wait()
 
     def project(o):
         p = mm(r.g1[o], r.wqkv[...], NN)
         at = pl.ds(pl.multiple_of(o * R, R), R)
-        q = (p[:, :HW] + r.vec[6:7, head_lanes]).astype(BF16)
-        k = p[:, HW : 2 * HW].astype(BF16)
-        v = (p[:, 2 * HW :] + r.vec[7:8, head_lanes]).astype(BF16)
-        r.qkv[at, 0:HW] = q
-        r.qkv[at, HW : 2 * HW] = k
-        r.qkv[at, 2 * HW :] = v
-        r.qT[:, at] = q.T
-        r.kT[:, at] = k.T
-        r.vT[:, at] = v.T
+        for pair in range(PAIRS):
+            rows = slice(pair * PAIR, (pair + 1) * PAIR)
+            lanes = pl.ds(pl.multiple_of(m * HW + pair * PAIR, PAIR), PAIR)
+            q, k, v = (p[:, qkv_lanes(pair, kind)] for kind in range(3))
+            q = (q + r.vec[6:7, lanes]).astype(BF16)
+            k = k.astype(BF16)
+            v = (v + r.vec[7:8, lanes]).astype(BF16)
+            for kind, value in enumerate((q, k, v)):
+                r.qkv[at, qkv_lanes(pair, kind)] = value
+            r.qT[rows, at] = q.T
+            r.kT[rows, at] = k.T
+            r.vT[rows, at] = v.T
 
     project(m)
     count_next()
     for j in range(C):
         ag[j][1].wait()
     project(mc)
-    count_next()
+    for _ in range(1, dp_size.bit_length() - 1):
+        count_next()
     fw = {}
     for j in range(C):
         ag[j][0].wait()
@@ -535,12 +684,15 @@
         return jnp.exp2(head.astype(F32) * (-8.0 / HEADS)) * log2_e
 
     def pair_lanes(h, start):
-        return pl.ds(pl.multiple_of(start + (h // 2) * 2 * HD, 2 * HD), 2 * HD)
+        return pl.ds(pl.multiple_of(start + (h // 2) * PAIR, PAIR), PAIR)
+
+    def kind_lanes(h, kind):
+        return pl.ds(pl.multiple_of((h // 2) * 3 * PAIR + kind * PAIR, PAIR), PAIR)
 
     def head_scores(i, ke, h):
         mask = (pair_row == lax.rem(h, 2)).astype(F32).astype(BF16)
         q_cols = r.qT[pair_lanes(h, 0), i * BQ : (i + 1) * BQ] * mask
-        raw = mm(r.qkv[0:ke, pair_lanes(h, HW)], q_cols, NN)
+        raw = mm(r.qkv[0:ke, kind_lanes(h, 1)], q_cols, NN)
         return raw * scale2 - head_slope(h) * r.big[0 : i + 1, :, DIST : DIST + BQ].reshape(ke, BQ)
 
     n_blocks = T // BQ
@@ -560,12 +712,10 @@
             r.mixT[at, :] = mm(r.vT[at, 0:ke], p, NN).astype(BF16)
             return carry
 
-        lax.fori_loop(0, LOCAL_HEADS, head_body, 0)
+        lax.fori_loop(0, LOCAL_HEADS, head_body, 0, unroll=True)
         r.mix[block, :] = r.mixT[...].T
-        if i < len(bits) - 2:
+        if i < mp_size.bit_length() - 1:
             count_next()
-    for _ in range(2 + n_blocks, len(bits)):
-        count_next()
 
     def rows4(ref, j):
         v = ref[:, pl.ds(j * rc, rc), :]
@@ -592,7 +742,7 @@
         ag[j][1].wait()
         cf.wait()
 
-    weights[1].wait()
+    weights[0].wait()
     rs = {}
     for j in range(C):
         rs[j] = rs_start(0, j, pair_flat(r.mix, j), lambda lanes: (r.wout[:, lanes], NN))
@@ -605,8 +755,8 @@
         r.inv2[rows, :] = inverse
         ag[j] = ag_start(1, j, r.g2, (normed * r.vec[3:4, :] + r.vec[4:5, :]).astype(BF16))
 
+    weights[1].wait()
     weights[2].wait()
-    weights[3].wait()
     for j in range(C):
         ag_finish(1, j, r.g2)
         rows = rows4(r.g2, j)
@@ -627,15 +777,16 @@
         rows = slice(j * rc, (j + 1) * rc)
         out = r.hidden[rows, :] + rs_finish(j, rs[j]) + r.vec[5:6, :]
         r.bo[rows, :] = out.astype(BF16)
-        grad = r.valid[rows, :] * (out - r.t[rows, :].astype(F32)) * loss_scale
+        valid = jnp.broadcast_to(r.valid[:, rows].astype(F32), (SHARE, rc)).T[:, 0:1]
+        grad = valid * (out - r.t[rows, :].astype(F32)) * loss_scale
         r.ig[rows, :] = grad
         ag[j] = ag_start(2, j, r.g3, grad.astype(BF16))
         r.vg[5:6, :] += jnp.sum(grad, 0, keepdims=True)
 
     for j in range(C):
         ag_finish(2, j, r.g3)
-        if fast and j == C - 1:
-            y_start("d")
+        if j == C - 1:
+            turn("third rows")
         rows = rows4(r.g3, j)
 
         def act_body(n, carry):
@@ -670,9 +821,8 @@
         r.vg[3:4, :] += jnp.sum(gs * r.n2[rows, :], 0, keepdims=True)
         r.vg[4:5, :] += jnp.sum(gs, 0, keepdims=True)
 
-    if fast:
-        y_start("u")
-    else:
+    turn("second norm")
+    if not fast:
         whole_grad(r.g2, r.gup, FU, r.u_grad)
     r.vg[pl.ds(8 + m, 1), :] = jnp.sum(r.gup[...].reshape(T, FU).astype(F32), 0, keepdims=True)
 
@@ -687,45 +837,54 @@
         return carry
 
     lax.fori_loop(0, mp_size, gm_body, 0)
-    if fast:
-        y_start("o")
+    turn("fourth rows")
 
     r.big[:, :, K_AT : K_AT + HW] = jnp.zeros((mp_size, R, HW), F32)
     r.big[:, :, V_AT : V_AT + HW] = jnp.zeros((mp_size, R, HW), F32)
-    for i in range(n_blocks):
-        ke = (i + 1) * BQ
-        block = slice(i * BQ, (i + 1) * BQ)
-        make_dist(i)
-
-        def back_body(h, carry):
-            lanes = pair_lanes(h, 0)
-            row_mask = (pair_row == lax.rem(h, 2)).astype(F32).astype(BF16)
-            lane_mask = (pair_lane == lax.rem(h, 2)).astype(F32).astype(BF16)
-            p = jnp.exp2(head_scores(i, ke, h) - r.lse[h, :, block])
-            gp = mm(r.qkv[0:ke, pair_lanes(h, 2 * HW)], r.vT[lanes, block] * row_mask, NN)
-            inner = jnp.sum(p * gp, 0, keepdims=True)
-            raw = (p * (gp - inner)).astype(BF16)
-            low = p.astype(BF16)
-            r.big[0 : i + 1, :, pair_lanes(h, V_AT)] += mm(
-                low, r.gm[block, lanes] * lane_mask, NN
-            ).reshape(i + 1, BQ, 2 * HD)
-            r.big[0 : i + 1, :, pair_lanes(h, K_AT)] += mm(
-                raw, r.qkv[block, lanes] * lane_mask, NN
-            ).reshape(i + 1, BQ, 2 * HD)
-            at = pl.ds(pl.multiple_of(h * HD, HD), HD)
-            r.big[i, at, Q_AT : Q_AT + BQ] = mm(r.kT[at, 0:ke], raw, NN) * (1.0 / math.sqrt(HD))
-            return carry
-
-        lax.fori_loop(0, LOCAL_HEADS, back_body, 0)
-        r.st[block, 0:HW] = r.big[i, 0:HW, Q_AT : Q_AT + BQ].T.astype(BF16)
-        if fast and i >= 1:
-            chain_step("d", i - 1)
-    r.st[:, HW : 2 * HW] = (
-        r.big[:, :, K_AT : K_AT + HW].reshape(T, HW) * (1.0 / math.sqrt(HD))
-    ).astype(BF16)
-    r.st[:, 2 * HW :] = r.big[:, :, V_AT : V_AT + HW].reshape(T, HW).astype(BF16)
-    r.vg[6:7, head_lanes] = jnp.sum(r.st[:, 0:HW].astype(F32), 0, keepdims=True)
-    r.vg[7:8, head_lanes] = jnp.sum(r.st[:, 2 * HW :].astype(F32), 0, keepdims=True)
+    for pair in range(PAIRS):
+        for i in range(n_blocks):
+            ke = (i + 1) * BQ
+            block = slice(i * BQ, (i + 1) * BQ)
+            make_dist(i)
+
+            def back_body(half, carry):
+                h = 2 * pair + half
+                row_mask = (pair_row == half).astype(F32).astype(BF16)
+                lane_mask = (pair_lane == half).astype(F32).astype(BF16)
+                lanes = slice(pair * PAIR, (pair + 1) * PAIR)
+                p = jnp.exp2(head_scores(i, ke, h) - r.lse[h, :, block])
+                gp = mm(r.qkv[0:ke, qkv_lanes(pair, 2)], r.vT[lanes, block] * row_mask, NN)
+                inner = jnp.sum(p * gp, 0, keepdims=True)
+                raw = (p * (gp - inner)).astype(BF16)
+                low = p.astype(BF16)
+                r.big[0 : i + 1, :, V_AT + lanes.start : V_AT + lanes.stop] += mm(
+                    low, r.gm[block, lanes] * lane_mask, NN
+                ).reshape(i + 1, BQ, PAIR)
+                r.big[0 : i + 1, :, K_AT + lanes.start : K_AT + lanes.stop] += mm(
+                    raw, r.qkv[block, qkv_lanes(pair, 0)] * lane_mask, NN
+                ).reshape(i + 1, BQ, PAIR)
+                at = pl.ds(pl.multiple_of(h * HD, HD), HD)
+                r.big[i, at, Q_AT : Q_AT + BQ] = mm(r.kT[at, 0:ke], raw, NN) * (1.0 / math.sqrt(HD))
+                return carry
+
+            lax.fori_loop(0, 2, back_body, 0)
+            rows = slice(pair * PAIR, (pair + 1) * PAIR)
+            r.st[block, qkv_lanes(pair, 0)] = r.big[i, rows, Q_AT : Q_AT + BQ].T.astype(BF16)
+            turn("block %d %d" % (pair, i))
+        lanes = slice(pair * PAIR, (pair + 1) * PAIR)
+        r.st[:, qkv_lanes(pair, 1)] = (
+            r.big[:, :, K_AT + lanes.start : K_AT + lanes.stop].reshape(T, PAIR) * (1.0 / math.sqrt(HD))
+        ).astype(BF16)
+        r.st[:, qkv_lanes(pair, 2)] = (
+            r.big[:, :, V_AT + lanes.start : V_AT + lanes.stop].reshape(T, PAIR).astype(BF16)
+        )
+        turn("pair %d" % pair)
+    for pair in range(PAIRS):
+        lanes = pl.ds(pl.multiple_of(m * HW + pair * PAIR, PAIR), PAIR)
+        for row, kind in ((6, 0), (7, 2)):
+            r.vg[row : row + 1, lanes] = jnp.sum(
+                r.st[:, qkv_lanes(pair, kind)].astype(F32), 0, keepdims=True
+            )
 
     if fast:
         fetch_state("u")
@@ -734,11 +893,8 @@
     for j in range(C):
         rs[j] = rs_start(3, j, pair_flat(r.st, j), lambda lanes: (r.wqkv[lanes, :], NT))
 
-    if fast:
-        y_start("q")
-        chain_step("u", 0)
-        finish_share("d")
-    else:
+    turn("projections back")
+    if not fast:
         whole_grad(r.mix, r.g4, D, r.o_grad)
         whole_grad(r.g1, r.st, 3 * HW, r.q_grad)
 
@@ -750,46 +906,58 @@
         r.vg[0:1, :] += jnp.sum(gf * normed, 0, keepdims=True)
         r.vg[1:2, :] += jnp.sum(gf, 0, keepdims=True)
 
-    vector_send, vector_next = doubling(r.vs, r.vs_r, r.vs_ss, r.vs_rs)
+    vector_send, vector_next = doubling(mp_bits + dp_bits, r.vs, r.vs_r, r.vs_ss, r.vs_rs)
     r.vs[0] = r.vg[...]
     vector_send(0)
+    late["vector_next"] = vector_next
+    turn("end")
     if fast:
-        chain_step("u", 1)
-        chain_step("o", 0)
-        vector_next()
-        gather_step("d", 1)
-        chain_step("u", 2)
-        chain_step("o", 1)
-        chain_step("q", 0)
-        vector_next()
-        finish_share("u")
-        gather_step("d", 2)
-        chain_step("o", 2)
-        chain_step("q", 1)
-        vector_next()
-        finish_share("o")
-        gather_step("d", 3)
-        gather_step("u", 1)
-        chain_step("q", 2)
-        gather_step("o", 1)
-        vector_next()
-        finish_share("q")
-        gather_step("u", 2)
-        gather_step("o", 2)
-        gather_step("q", 1)
-        gather_step("u", 3)
-        gather_step("o", 3)
-        gather_step("q", 2)
-        vector_next()
-        gather_step("q", 3)
-        for name in ("d", "u", "o", "q"):
+        for name in parts:
             gather_end(name)
         for cp in local_out:
             cp.wait()
     else:
         for _ in bits:
             vector_next()
-    r.vsum[...] = r.vs[len(bits)]
+    rows = r.vec.shape[0]
+    total = r.vs[len(bits), 0:rows]
+    r.v_grad[...] = total
+    new = adam_step(total, r.vec_state[0], r.vec_state[1], r.vec_state[2], 0.0, token_total)
+    for k in range(3):
+        r.v_new[k] = new[k]
+    r.v_low[...] = new[0].astype(BF16)
+
+
+Z_FIRST = ("d0",)
+Y_FIRST = ("u1",)
+ORDER = {
+    "third rows": "yd1 c0d0",
+    "second norm": "yu0 c0d1 c1d0 yu1 c1d1 c2d0",
+    "block 0 0": "yo0 c0u0",
+    "block 0 2": "c2d1",
+    "block 0 3": "c0u1",
+    "pair 0": "ed0 c1u0",
+    "block 1 1": "yq0 c1u1 fd1",
+    "block 1 2": "fd0",
+    "block 1 3": "c2u1",
+    "pair 1": "c2u0",
+    "projections back": "yq1 g1d0 c0q0 g1d1 c1q0 c0o0 g2d0 fu0 c1o0 g3d0 c2q0 c0q1 fu1 g1u0",
+    "end": """
+c1q1 c2o0 g2d1 g3d1 g2u0 c2q1 fq0 g3u0 v hu1
+fq1 fo0 v g1u1 g1q0 g1q1 g1o0 v g2q1 g2q0
+g2o0 v g3q1 g2u1 g3o0 v g3q0 g3u1
+""",
+}
+
+
+def pieces(head_width, units):
+    return [
+        ("d0", units // 2),
+        ("d1", units // 2),
+        ("u0", units // 2),
+        ("u1", units // 2),
+        ("o0", head_width),
+    ] + [("q%d" % pair, 6 * HD) for pair in range(head_width // (2 * HD))]
 
 
 SHARE = 128
@@ -806,6 +974,7 @@
     rc = R // C
     n_bits = (dp_size * mp_size).bit_length() - 1
     NZ = dp_size // 2
+    PAIRS = HW // (2 * HD)
     fast = D == dp_size * SHARE
     dma = pltpu.SemaphoreType.DMA
     V = pltpu.VMEM
@@ -816,9 +985,10 @@
     ins = {
         "x": (x, vmem),
         "t": (teacher, vmem),
-        "segr": (segments.reshape(1, T), vmem),
-        "valid": (valid.reshape(R, 1), vmem),
-        "vec": (vectors, vmem),
+        "segr": (segments, vmem),
+        "valid": (valid.reshape(1, R), vmem),
+        "vec_low": (vectors, vmem),
+        "vec_state": (states[4], vmem),
         "wqkv_hbm": (wqkv, anywhere),
         "wout_hbm": (wout, anywhere),
         "wup_hbm": (wup, anywhere),
@@ -827,11 +997,13 @@
     outs = {
         "bo": (S((R, D), BF16), vmem),
         "ig": (S((R, D), F32), vmem),
-        "vsum": (S((16, D), F32), vmem),
+        "v_grad": (S(vectors.shape, F32), vmem),
+        "v_new": (S(states[4].shape, F32), vmem),
+        "v_low": (S(vectors.shape, BF16), vmem),
     }
     if fast:
-        shard = {"q": (SHARE, 3 * HW), "o": (HW, SHARE), "u": (SHARE, FU), "d": (FU, SHARE)}
-        whole = {"q": (D, 3 * HW), "o": (HW, D), "u": (D, FU), "d": (FU, D)}
+        shard = {"q": (3, SHARE, HW), "o": (HW, SHARE), "u": (SHARE, FU), "d": (FU, SHARE)}
+        whole = {"q": (3, D, HW), "o": (HW, D), "u": (D, FU), "d": (FU, D)}
         for name, state in zip("qoud", states):
             ins["s%s_hbm" % name] = (state, anywhere)
         for name in "qoud":
@@ -850,7 +1022,9 @@
         "wout": V((HW, D), BF16),
         "wup": V((D, FU), BF16),
         "wdown": V((FU, D), BF16),
-        "w_sem": dma((4,)),
+        "w_sem": dma((3,)),
+        "wq_sem": dma((PAIRS, 3)),
+        "vec": V(vectors.shape, F32),
         "g1": V((mp_size, R, D), BF16),
         "g2": V((mp_size, R, D), BF16),
         "g3": V((mp_size, R, D), BF16),
@@ -891,28 +1065,31 @@
         "vs_rs": dma((n_bits,)),
     }
     if fast:
-        wide = {"q": 3 * HW, "o": HW, "u": FU, "d": FU}
+        for name, w in pieces(HW, FU):
+            shares = 1 if name in Z_FIRST else NZ
+            rows = 2 * SHARE if name in Z_FIRST else SHARE
+            scratch["ys" + name] = V((shares, SHARE, w), BF16)
+            scratch["yr" + name] = V((shares, SHARE, w), BF16)
+            scratch["zs" + name] = V((2, rows, w), BF16)
+            scratch["zr" + name] = V((2, NZ - 1, rows, w), BF16)
         for name in "qoud":
-            w = wide[name]
-            scratch["ys" + name] = V((NZ, SHARE, w), BF16)
-            scratch["yr" + name] = V((NZ, SHARE, w), BF16)
-            scratch["zs" + name] = V((2, SHARE, w), BF16)
-            scratch["zr" + name] = V((2, NZ - 1, SHARE, w), BF16)
-            if name in "od":
-                scratch["s" + name] = V((3,) + shard[name], F32)
             scratch["gr" + name] = V(shard[name], F32)
             scratch["nc" + name] = V(shard[name], BF16)
-        scratch["acc"] = V((SHARE, FU), F32)
-        scratch["s_sem"] = dma((4,))
-        scratch["o_sem"] = dma((4, 3))
-        scratch["y_ss"] = dma((4, NZ))
-        scratch["y_rs"] = dma((4, NZ))
-        scratch["z_ss"] = dma((4, 2, NZ - 1))
-        scratch["z_rs"] = dma((4, 2, NZ - 1))
-        scratch["az_ss"] = dma((4, 2, NZ - 1))
-        scratch["az_rs"] = dma((4, 2, NZ - 1))
-        scratch["ay_ss"] = dma((4, NZ))
-        scratch["ay_rs"] = dma((4, NZ))
+        scratch["sd"] = V((3,) + shard["d"], F32)
+        scratch["so"] = V((3,) + shard["o"], F32)
+        scratch["acc"] = V((SHARE, FU // 2), F32)
+        scratch["wide"] = V((2 * SHARE, FU // 2), F32)
+        n = len(pieces(HW, FU))
+        scratch["s_sem"] = dma((n, 3))
+        scratch["o_sem"] = dma((n, 5))
+        scratch["y_ss"] = dma((n, NZ))
+        scratch["y_rs"] = dma((n, NZ))
+        scratch["z_ss"] = dma((n, 2, NZ - 1))
+        scratch["z_rs"] = dma((n, 2, NZ - 1))
+        scratch["az_ss"] = dma((n, 2, 2, NZ - 1))
+        scratch["az_rs"] = dma((n, 2, 2, NZ - 1))
+        scratch["ay_ss"] = dma((n, NZ))
+        scratch["ay_rs"] = dma((n, NZ))
     else:
         scratch["stage"] = V((TILE, D), F32)
         scratch["stage_sem"] = dma
@@ -928,7 +1105,39 @@
         ),
         name="block",
     )(*[v[0] for v in ins.values()])
-    return dict(zip(outs, results)), fast
+    outs = dict(zip(outs, results))
+    if fast:
+        names, results = list(outs), list(outs.values())
+        outs = dict(zip(names, settle(results)))
+    return outs, fast
+
+
+def settle_kernel(count, *refs):
+    sources, results, held = refs[:count], refs[count : 2 * count], refs[2 * count : 3 * count]
+    in_sem, out_sem = refs[3 * count :]
+    loads = [pltpu.make_async_copy(sources[i], held[i], in_sem.at[i]) for i in range(count)]
+    stores = [pltpu.make_async_copy(held[i], results[i], out_sem.at[i]) for i in range(count)]
+    for cp in loads:
+        cp.start()
+    for load, store in zip(loads, stores):
+        load.wait()
+        store.start()
+    for cp in stores:
+        cp.wait()
+
+
+def settle(arrays):
+    anywhere = pl.BlockSpec(memory_space=pltpu.HBM)
+    dma = pltpu.SemaphoreType.DMA((len(arrays),))
+    return pl.pallas_call(
+        functools.partial(settle_kernel, len(arrays)),
+        out_shape=[jax.ShapeDtypeStruct(a.shape, a.dtype) for a in arrays],
+        in_specs=[anywhere] * len(arrays),
+        out_specs=[anywhere] * len(arrays),
+        scratch_shapes=[pltpu.VMEM(a.shape, a.dtype) for a in arrays] + [dma, dma],
+        compiler_params=pltpu.CompilerParams(vmem_limit_bytes=62 << 20),
+        name="settle",
+    )(*arrays)
 
 
 def adam_update(gradient, stored, decay_factor, token_total):
@@ -956,32 +1165,28 @@
     token_total = inputs.shape[0] * sizes[0] * sizes[1]
     width = inputs.shape[1]
     head_width = qkv_copy.shape[2]
+    pairs = head_width // (2 * HD)
     outs, fast = block_call(
         sizes,
         inputs,
         teacher,
         segments,
-        valid_mask.astype(F32),
-        vector_copy.astype(F32),
-        (qkv_copy.reshape(width, 3 * head_width), out_copy, up_copy, down_copy),
-        (
-            qkv_state.reshape(qkv_state.shape[:2] + (3 * head_width,)),
-            out_state,
-            up_state,
-            down_state,
-        ),
+        valid_mask,
+        vector_copy,
+        (qkv_copy.transpose(1, 0, 2), out_copy, up_copy, down_copy),
+        (qkv_state.transpose(0, 2, 1, 3), out_state, up_state, down_state, vector_state),
     )
-    vector_grad = outs["vsum"][: vector_copy.shape[0]]
-    vector_new, vector_low = adam_update(vector_grad, vector_state, 0.0, token_total)
+    vector_grad, vector_new, vector_low = outs["v_grad"], outs["v_new"], outs["v_low"]
     if fast:
-        qkv_grad = outs["q_grad"].reshape(qkv_state.shape[1:])
+        qkv_grad = outs["q_grad"].transpose(1, 0, 2)
         out_grad, up_grad, down_grad = (outs[n + "_grad"] for n in "oud")
-        qkv_new = outs["q_new"].reshape(qkv_state.shape)
+        qkv_new = outs["q_new"].transpose(0, 2, 1, 3)
         out_new, up_new, down_new = (outs[n + "_new"] for n in "oud")
-        qkv_full = outs["q_full"].reshape(qkv_copy.shape)
+        qkv_full = outs["q_full"].transpose(1, 0, 2)
         out_full, up_full, down_full = (outs[n + "_full"] for n in "oud")
     else:
-        qkv_local = outs["q_grad"].reshape(width, 3, head_width)
+        qkv_local = outs["q_grad"].reshape(width, pairs, 3, 2 * HD)
+        qkv_local = qkv_local.transpose(0, 2, 1, 3).reshape(width, 3, head_width)
         qkv_grad, out_grad, up_grad, down_grad = (
             lax.psum_scatter(qkv_local, "dp", scatter_dimension=0, tiled=True),
             lax.psum_scatter(outs["o_grad"], "dp", scatter_dimension=1, tiled=True),

time: 275 us -> 240 us (0.87)
  local copies, waits for them, and re-layouts: 25.5 us -> 0 us
  Pallas kernels: 244 us -> 236 us
  other arithmetic: 4.4 us -> 0 us
    unnamed x48 -> x0, local copies, waits for them, and re-layouts: 19.5 us -> none
    pallas_call x1, Pallas kernels: 244 us -> 226 us  [block_call(): pl.pallas_call(functools.partial(block_kernel, sizes, fast, names), out_s...]
    pallas_call x0 -> x1, Pallas kernels: none -> 10.6 us  [settle(): pl.pallas_call(functools.partial(settle_kernel, len(arrays)), out_shape=[...]
    reshape x3 -> x0, local copies, waits for them, and re-layouts: 3.75 us -> none  [the longest x1 1.57 us: shards(): qkv_copy.reshape(width, 3 * head_width)]
    convert_element_type x3 -> x0, other arithmetic: 3.69 us -> none  [the longest x1 1.61 us: adam_update(): return (jnp.stack(new), new[0].astype(jnp.bfloat16))]
where the time goes in v3:
time: 240 us; the launch traced here: 237 us
  Pallas kernels  236 us (98%)
    pallas_call x1, Pallas kernels, block_call(): pl.pallas_call(functools.partial(block_kernel, sizes, fast, names), out_s...  226 us
    pallas_call x1, Pallas kernels, settle(): pl.pallas_call(functools.partial(settle_kernel, len(arrays)), out_shape=[...  10.6 us

profile of v3, /device:TPU:0, one launch (start us, length us, event | category | flops | bytes accessed | tf_op | source)
XLA Modules:
  0.0 237.0 jit_solution(17229519471774865719)
XLA Ops:
  0.7 225.6 %block.1 = (bf16[256,1024]{1,0:T(8,128)(2,1)}, f32[256,1024]{1,0:T(8,128)}, f32[12,1024]{1,0:T(8,128)}, f32[3,12,1024]{2,1,0:T(8,128)}, bf16[12,1024]{1,0:T(8,12...) custom-call(bf16[256,1024]{1,0:T(8,128)(2,1)} %refs_0_.1, ...), custom_call_target="tpu_custom_call" | custom-call | tf_op jit(solution)/shard_map/block/pallas_call | solution.py:1097
  226.3 10.6 %settle.1 = (bf16[256,1024]{1,0:T(8,128)(2,1)}, f32[256,1024]{1,0:T(8,128)}, f32[12,1024]{1,0:T(8,128)}, f32[3,12,1024]{2,1,0:T(8,128)}, bf16[12,1024]{1,0:T(8,1...) custom-call(bf16[256,1024]{1,0:T(8,128)(2,1)} %get-tuple-element.51., ...), custom_call_target="tpu_custom_call" | custom-call | tf_op jit(solution)/shard_map/settle/pallas_call | solution.py:1132
